TPU v7x, 32 devices: a whole 2x2x4 slice. The times are simulated.
32 devices in a mesh: dp: 8 (over z, y), mp: 4 (over x, core).
Axes of the slice: x: 2, y: 2, z: 4, core: 2. Of those that a mesh axis runs over, the one named last changes fastest.
Arguments:
- token_ids: int32 [4096], P('dp'), may hold values from 0 to 127
- prefix_lengths: int32 [8], P('dp'), may hold values from 1 to 511
- cluster_ids: int32 [8], replicated, may hold values from 0 to 3
- embedding: bfloat16 [128, 2048], replicated, may hold values from -6 to 6
- w_query: bfloat16 [2048, 2048], P(None, 'mp'), may hold values from -0.125 to 0.125
- w_key: bfloat16 [2048, 2048], P(None, 'mp'), may hold values from -0.125 to 0.125
- w_value: bfloat16 [2048, 2048], P(None, 'mp'), may hold values from -0.125 to 0.125
- w_dense: bfloat16 [2048, 2048], P(None, 'mp'), may hold values from -6 to 6
- w_gate: bfloat16 [2048, 5472], P(None, 'mp'), may hold values from -0.125 to 0.125
- w_up: bfloat16 [2048, 5472], P(None, 'mp'), may hold values from -0.125 to 0.125
- w_down: bfloat16 [2048, 5472], P(None, 'mp'), may hold values from -0.75 to 0.75
- norm1_gain: float32 [2048], replicated, may hold values from 0.5 to 1.5
- norm1_bias: float32 [2048], replicated, may hold values from -4 to 4
- norm2_gain: float32 [2048], replicated, may hold values from 0.5 to 1.5
- norm2_bias: float32 [2048], replicated, may hold values from -4 to 4
- cotangent: bfloat16 [4096, 2048], P('dp'), may hold values from -6 to 6
Outputs:
- block_out: bfloat16 [4096, 2048], P('dp')
- grad_embedding: float32 [128, 2048], P('dp')
- grad_w_query: float32 [2048, 2048], P('dp', 'mp')
- grad_w_key: float32 [2048, 2048], P('dp', 'mp')
- grad_w_value: float32 [2048, 2048], P('dp', 'mp')
- grad_w_dense: float32 [2048, 2048], P('dp', 'mp')
- grad_w_gate: float32 [2048, 5472], P('dp', 'mp')
- grad_w_up: float32 [2048, 5472], P('dp', 'mp')
- grad_w_down: float32 [2048, 5472], P('dp', 'mp')
- grad_norm1_gain: float32 [2048], P('dp')
- grad_norm1_bias: float32 [2048], P('dp')
- grad_norm2_gain: float32 [2048], P('dp')
- grad_norm2_bias: float32 [2048], P('dp')
All inputs are finite; a program needn't handle non-finite values.
Results may differ from a plain program's by a relative error of at most 0.014.
Values sent between devices are 32-bit elements; how exact they have to be, the bound alone decides.
A program may use at most 192 MiB of HBM per device.

v0:
```python
import math

import jax
import jax.numpy as jnp
from jax import lax
from jax.sharding import PartitionSpec as P

HD = 128
FF_USED = 5461


deep_alpha = math.sqrt(48.0)
norm_eps = 1e-05
highest = lax.Precision.HIGHEST


def layer_norm(inputs, norm_gain, norm_bias):
    center = jnp.mean(inputs, axis=-1, keepdims=True)
    centered = inputs - center
    spread = jnp.mean(centered * centered, axis=-1, keepdims=True)
    return centered * lax.rsqrt(spread + norm_eps) * norm_gain + norm_bias


def rotary_tables(length, head_width):
    half_width = head_width // 2
    frequency = jnp.exp(
        jnp.arange(half_width, dtype=jnp.float32) * (-2.0 * math.log(10000.0) / head_width)
    )
    angles = jnp.arange(length, dtype=jnp.float32)[:, None] * frequency[None, :]
    return (jnp.cos(angles), jnp.sin(angles))


def rotate(inputs, cosine, sine):
    half_width = inputs.shape[-1] // 2
    first = inputs[..., :half_width]
    second = inputs[..., half_width:]
    cosine = cosine[:, None, :]
    sine = sine[:, None, :]
    return jnp.concatenate(
        [first * cosine - second * sine, second * cosine + first * sine], axis=-1
    )


def row_mask(row_begin, row_count, length, prefix):
    columns = jnp.arange(length, dtype=jnp.int32)
    row_index = row_begin + jnp.arange(row_count, dtype=jnp.int32)
    return (columns[None, :] < prefix) | (columns[None, :] <= row_index[:, None])


def block_scores(query_block, keys_rot, visible, score_scale):
    scores = (
        jnp.einsum("bhd,khd->hbk", query_block, keys_rot, preferred_element_type=jnp.float32)
        * score_scale
    )
    return jnp.where(visible[None, :, :], scores, -1e30)


def attention_forward(queries, keys_rot, values_in, prefix, row_block):
    length = queries.shape[0]
    score_scale = 1.0 / math.sqrt(HD)

    def one_block(row_begin):
        scores = block_scores(
            queries, keys_rot, row_mask(row_begin, row_block, length, prefix), score_scale
        )
        row_max = jnp.max(scores, axis=-1, keepdims=True)
        weights = jnp.exp(scores - row_max)
        total_weight = jnp.sum(weights, axis=-1, keepdims=True)
        probability = (weights / total_weight).astype(jnp.bfloat16)
        mixed_block = jnp.einsum(
            "hbk,khd->bhd", probability, values_in, preferred_element_type=jnp.float32
        )
        return (mixed_block, row_max + jnp.log(total_weight))

    starts = jnp.arange(length // row_block, dtype=jnp.int32) * row_block
    attended, log_total = lax.map(one_block, starts)
    return (attended.reshape(length, -1), log_total)


def attention_backward(queries, keys_rot, values_in, prefix, row_block, log_total, grad_mixed):
    length = queries.shape[0]
    score_scale = 1.0 / math.sqrt(HD)

    def one_block(carried, inputs):
        grad_keys, grad_values = carried
        row_begin, block_total = inputs
        scores = block_scores(
            queries, keys_rot, row_mask(row_begin, row_block, length, prefix), score_scale
        )
        probability = jnp.exp(scores - block_total)
        prob_low = probability.astype(jnp.bfloat16)
        grad_prob = jnp.einsum(
            "bhd,khd->hbk", grad_mixed, values_in, preferred_element_type=jnp.float32
        )
        centre = jnp.sum(grad_prob * probability, axis=-1, keepdims=True)
        grad_scores = (probability * (grad_prob - centre)).astype(jnp.bfloat16)
        grad_query = (
            jnp.einsum("hbk,khd->bhd", grad_scores, keys_rot, preferred_element_type=jnp.float32)
            * score_scale
        )
        grad_keys = (
            grad_keys
            + jnp.einsum("hbk,bhd->khd", grad_scores, queries, preferred_element_type=jnp.float32)
            * score_scale
        )
        grad_values = grad_values + jnp.einsum(
            "hbk,bhd->khd", prob_low, grad_mixed, preferred_element_type=jnp.float32
        )
        return ((grad_keys, grad_values), grad_query)

    starts = jnp.arange(length // row_block, dtype=jnp.int32) * row_block
    zeros_kv = jnp.zeros(keys_rot.shape, jnp.float32)
    (grad_keys, grad_values), grad_queries = lax.scan(
        one_block, (zeros_kv, zeros_kv), (starts, log_total)
    )
    return (grad_queries.reshape(queries.shape), grad_keys, grad_values)


def local(
    token_ids,
    prefix_lengths,
    cluster_ids,
    embedding,
    w_query,
    w_key,
    w_value,
    w_dense,
    w_gate,
    w_up,
    w_down,
    norm1_gain,
    norm1_bias,
    norm2_gain,
    norm2_bias,
    cotangent,
):
    length = token_ids.shape[0]
    vocab_rows = embedding.shape[0]
    row_block = min(512, length)
    local_heads = w_query.shape[1] // HD
    local_hidden = w_gate.shape[1]
    one_hot = (token_ids[:, None] == jnp.arange(vocab_rows, dtype=jnp.int32)[None, :]).astype(
        jnp.bfloat16
    )
    embedded_low = jnp.dot(one_hot, embedding, preferred_element_type=jnp.float32).astype(
        jnp.bfloat16
    )
    embedded = embedded_low.astype(jnp.float32)
    cosine, sine = rotary_tables(length, HD)
    prefix = prefix_lengths[0]
    own_cluster = cluster_ids[lax.axis_index("dp")]
    seq_weight = 1.0 / jnp.sum((cluster_ids == own_cluster).astype(jnp.float32))

    def project(weight_in):
        return jnp.dot(embedded_low, weight_in, preferred_element_type=jnp.float32).reshape(
            length, local_heads, HD
        )

    queries = rotate(project(w_query), cosine, sine).astype(jnp.bfloat16)
    keys_rot = rotate(project(w_key), cosine, sine).astype(jnp.bfloat16)
    values_in = project(w_value).astype(jnp.bfloat16)
    attended, log_total = attention_forward(queries, keys_rot, values_in, prefix, row_block)
    attended_low = attended.astype(jnp.bfloat16)
    branch = lax.psum(
        jnp.einsum("lh,dh->ld", attended_low, w_dense, preferred_element_type=jnp.float32), "mp"
    )
    residual_one = deep_alpha * embedded + branch
    hidden, norm_one_pull = jax.vjp(layer_norm, residual_one, norm1_gain, norm1_bias)
    hidden_low = hidden.astype(jnp.bfloat16)
    gate_proj = jnp.dot(hidden_low, w_gate, preferred_element_type=jnp.float32)
    up_proj = jnp.dot(hidden_low, w_up, preferred_element_type=jnp.float32)
    unit_index = lax.axis_index("mp") * local_hidden + jnp.arange(local_hidden, dtype=jnp.int32)
    used_mask = (unit_index < FF_USED).astype(jnp.float32)

    def gated_unit(gate_in, up_in):
        return jax.nn.gelu(gate_in, approximate=True) * up_in * used_mask

    activation, gated_pull = jax.vjp(gated_unit, gate_proj, up_proj)
    activation_low = activation.astype(jnp.bfloat16)
    branch_two = lax.psum(
        jnp.einsum("lf,df->ld", activation_low, w_down, preferred_element_type=jnp.float32), "mp"
    )
    residual_two = deep_alpha * hidden + branch_two
    final, norm_two_pull = jax.vjp(layer_norm, residual_two, norm2_gain, norm2_bias)
    grad_out = cotangent.astype(jnp.float32) * seq_weight
    grad_two, grad_gain_two, grad_bias_two = norm_two_pull(grad_out)
    grad_branch_two = grad_two.astype(jnp.bfloat16)
    grad_w_down = jnp.einsum(
        "ld,lf->df", grad_branch_two, activation_low, preferred_element_type=jnp.float32
    )
    grad_act = jnp.dot(grad_branch_two, w_down, preferred_element_type=jnp.float32)
    grad_gate, grad_up = gated_pull(grad_act)
    grad_gate_low = grad_gate.astype(jnp.bfloat16)
    grad_up_low = grad_up.astype(jnp.bfloat16)
    grad_w_gate = jnp.einsum(
        "ld,lf->df", hidden_low, grad_gate_low, preferred_element_type=jnp.float32
    )
    grad_w_up = jnp.einsum("ld,lf->df", hidden_low, grad_up_low, preferred_element_type=jnp.float32)
    hidden_part = jnp.einsum(
        "lf,df->ld", grad_gate_low, w_gate, preferred_element_type=jnp.float32
    ) + jnp.einsum("lf,df->ld", grad_up_low, w_up, preferred_element_type=jnp.float32)
    grad_hidden = deep_alpha * grad_two + lax.psum(hidden_part, "mp")
    feed_sums = (
        lax.psum_scatter(grad_w_gate, "dp", scatter_dimension=0, tiled=True),
        lax.psum_scatter(grad_w_up, "dp", scatter_dimension=0, tiled=True),
        lax.psum_scatter(grad_w_down, "dp", scatter_dimension=0, tiled=True),
        lax.psum_scatter(grad_gain_two, "dp", scatter_dimension=0, tiled=True),
        lax.psum_scatter(grad_bias_two, "dp", scatter_dimension=0, tiled=True),
    )
    grad_one, grad_gain_one, grad_bias_one = norm_one_pull(grad_hidden)
    grad_branch = grad_one.astype(jnp.bfloat16)
    grad_w_dense = jnp.einsum(
        "ld,lh->dh", grad_branch, attended_low, preferred_element_type=jnp.float32
    )
    grad_attended = jnp.dot(grad_branch, w_dense, preferred_element_type=jnp.float32).astype(
        jnp.bfloat16
    )
    grad_attended = grad_attended.reshape(length, local_heads, HD)
    grad_queries, grad_keys, grad_values = attention_backward(
        queries, keys_rot, values_in, prefix, row_block, log_total, grad_attended
    )
    grad_query_lin = rotate(grad_queries, cosine, -sine).astype(jnp.bfloat16).reshape(length, -1)
    grad_key_lin = rotate(grad_keys, cosine, -sine).astype(jnp.bfloat16).reshape(length, -1)
    grad_value_lin = grad_values.astype(jnp.bfloat16).reshape(length, -1)
    grad_w_query = jnp.einsum(
        "ld,lh->dh", embedded_low, grad_query_lin, preferred_element_type=jnp.float32
    )
    grad_w_key = jnp.einsum(
        "ld,lh->dh", embedded_low, grad_key_lin, preferred_element_type=jnp.float32
    )
    grad_w_value = jnp.einsum(
        "ld,lh->dh", embedded_low, grad_value_lin, preferred_element_type=jnp.float32
    )
    input_part = (
        jnp.einsum("lh,dh->ld", grad_query_lin, w_query, preferred_element_type=jnp.float32)
        + jnp.einsum("lh,dh->ld", grad_key_lin, w_key, preferred_element_type=jnp.float32)
        + jnp.einsum("lh,dh->ld", grad_value_lin, w_value, preferred_element_type=jnp.float32)
    )
    grad_embedded = deep_alpha * grad_one + lax.psum(input_part, "mp")
    grad_table = 0.1 * jnp.dot(one_hot.astype(jnp.float32).T, grad_embedded, precision=highest)
    attn_sums = (
        lax.psum_scatter(grad_table, "dp", scatter_dimension=0, tiled=True),
        lax.psum_scatter(grad_w_query, "dp", scatter_dimension=0, tiled=True),
        lax.psum_scatter(grad_w_key, "dp", scatter_dimension=0, tiled=True),
        lax.psum_scatter(grad_w_value, "dp", scatter_dimension=0, tiled=True),
        lax.psum_scatter(grad_w_dense, "dp", scatter_dimension=0, tiled=True),
        lax.psum_scatter(grad_gain_one, "dp", scatter_dimension=0, tiled=True),
        lax.psum_scatter(grad_bias_one, "dp", scatter_dimension=0, tiled=True),
    )
    summed = (
        attn_sums[0],
        attn_sums[1],
        attn_sums[2],
        attn_sums[3],
        attn_sums[4],
        feed_sums[0],
        feed_sums[1],
        feed_sums[2],
        attn_sums[5],
        attn_sums[6],
        feed_sums[3],
        feed_sums[4],
    )
    return (
        final.astype(jnp.bfloat16),
        summed[0],
        summed[1],
        summed[2],
        summed[3],
        summed[4],
        summed[5],
        summed[6],
        summed[7],
        summed[8],
        summed[9],
        summed[10],
        summed[11],
    )


def solution(mesh):
    return jax.shard_map(
        local,
        mesh=mesh,
        in_specs=(
            P("dp"),
            P("dp"),
            P(),
            P(),
            P(None, "mp"),
            P(None, "mp"),
            P(None, "mp"),
            P(None, "mp"),
            P(None, "mp"),
            P(None, "mp"),
            P(None, "mp"),
            P(),
            P(),
            P(),
            P(),
            P("dp", None),
        ),
        out_specs=(
            P("dp", None),
            P("dp", None),
            P("dp", "mp"),
            P("dp", "mp"),
            P("dp", "mp"),
            P("dp", "mp"),
            P("dp", "mp"),
            P("dp", "mp"),
            P("dp", "mp"),
            P("dp"),
            P("dp"),
            P("dp"),
            P("dp"),
        ),
        check_vma=False,
    )
```

profile of v0, /device:TPU:30, one launch (start us, length us, event | category | flops | bytes accessed | tf_op | source)
XLA Modules:
  0.0 1481.9 jit_solution(569187631338442900)
XLA Ops:
  7.3 1.9 convolution_convert_fusion
  9.2 4.5 convolution_convert_fusion.2
  13.7 1.3 fusion.54
  15.1 1.3 copy.86
  16.4 1.3 copy.85
  17.7 1.7 fusion.36
  19.5 3.5 fusion.55
  23.1 1.3 copy.87
  24.4 1.3 copy.88
  26.5 2.8 subtract_convert_fusion.3
  29.3 1.4 fusion.53
  31.3 0.9 fusion.30
  32.7 0.8 copy-done.18
  33.5 3.3 fusion.56
  37.1 85.5 %all-reduce.10.cloned.1.call-done = f32[512,2048]{1,0:T(8,128)} async-done(((f32[512,2048]{1,0:T(8,128)}), f32[512,2048]{1,0:T(8,128)}) %all-reduce.10.cloned.1.call-update) | async-done | bytes 4194320 | tf_op jit(solution)/shard_map/psum | solution.py:164
  122.6 3.6 fusion.50
  128.8 3.2 fusion.57
  132.0 5.5 multiply_convert_fusion.2
  137.5 1.1 copy-done.36
  138.6 5.0 fusion.58
  144.9 1.2 fusion.40
  146.9 82.6 %all-reduce.12.cloned.1.call-done = f32[512,2048]{1,0:T(8,128)} async-done(((f32[512,2048]{1,0:T(8,128)}), f32[512,2048]{1,0:T(8,128)}) %all-reduce.12.cloned.1.call-update) | async-done | bytes 4194320 | tf_op jit(solution)/shard_map/psum | solution.py:180
  229.5 4.6 fusion.49
  234.7 1.0 copy-done.11
  235.7 2.5 multiply_reduce_fusion
  238.3 3.1 fusion.48
  242.1 5.4 multiply_convert_fusion.1
  247.6 3.6 fusion.59
  251.3 5.0 convolution_add_fusion
  256.3 85.7 %all-reduce.14.cloned.1.call-done = f32[512,2048]{1,0:T(8,128)} async-done(((f32[512,2048]{1,0:T(8,128)}), f32[512,2048]{1,0:T(8,128)}) %all-reduce.14.cloned.1.call-update) | async-done | bytes 4194320 | tf_op jit(solution)/shard_map/psum | solution.py:202
  342.1 6.2 multiply_reduce_fusion.1
  348.3 1.2 fusion.47
  349.5 1.4 convolution_convert_fusion.1
  351.6 1.6 copy-done.5
  353.3 0.9 multiply_reduce_fusion.2
  354.3 1.2 multiply_convert_fusion
  355.5 0.8 fusion.25
  356.3 1.0 fusion.26
  357.4 0.8 fusion.27
  359.8 4.9 fusion.60
  364.9 3.0 fusion.61
  368.4 3.6 add_add_fusion.2
  372.1 85.7 %all-reduce.16.cloned.1.call-done = f32[512,2048]{1,0:T(8,128)} async-done(((f32[512,2048]{1,0:T(8,128)}), f32[512,2048]{1,0:T(8,128)}) %all-reduce.16.cloned.1.call-update) | async-done | bytes 4194320 | tf_op jit(solution)/shard_map/psum | solution.py:239
  457.8 6.6 fusion.16
  464.5 3.3 fusion.62
  467.9 3.3 fusion.63
  471.2 1.0 copy-done.17
  472.2 3.3 fusion.64
  475.6 1.0 copy-done.19
  476.5 5.7 fusion.46
  482.3 1.6 copy-done.22
  484.3 5.8 fusion.65
  490.2 1.3 copy-done.25
  491.5 5.7 fusion.66
  497.2 1.3 copy-done.37
  498.5 8.0 fusion.45
  508.6 32.6 %all-reduce.4 = (f32[2048]{0:T(1024)S(1)}, f32[2048]{0:T(1024)S(1)}, f32[2048]{0:T(1024)S(1)}, f32[2048]{0:T(1024)S(1)}) all-reduce(f32[2048]{0:T(1024)S(1)} %get-tuple-element.54, f32[2048]{0:T(1024)S(1)} %get-tuple-element.68, f32[2048]{0:T(1024)S(1)} %get-tuple-element.56, ...), channel_id=10, replica_groups=mesh['dp'=8,'mp'=4] {'dp'}, use_global_device_ids=true, to_apply=%region_25.26.clone | all-reduce | flops 8192 | bytes 65536
  543.7 75.4 %reduce-scatter.11.cloned.1.call-done = f32[256,512]{1,0:T(8,128)} async-done(((f32[2048,512]{1,0:T(8,128)}), f32[256,512]{1,0:T(8,128)}) %reduce-scatter.11.cloned.1.call-update) | async-done | bytes 524304 | tf_op jit(solution)/shard_map/reduce_scatter | solution.py:243
  619.1 91.9 %reduce-scatter.13.cloned.1.call-done = f32[256,512]{1,0:T(8,128)} async-done(((f32[2048,512]{1,0:T(8,128)}), f32[256,512]{1,0:T(8,128)}) %reduce-scatter.13.cloned.1.call-update) | async-done | bytes 524304 | tf_op jit(solution)/shard_map/reduce_scatter | solution.py:244
  711.0 92.5 %reduce-scatter.15.cloned.1.call-done = f32[256,512]{1,0:T(8,128)} async-done(((f32[2048,512]{1,0:T(8,128)}), f32[256,512]{1,0:T(8,128)}) %reduce-scatter.15.cloned.1.call-update) | async-done | bytes 524304 | tf_op jit(solution)/shard_map/reduce_scatter | solution.py:245
  803.6 92.1 %reduce-scatter.17.cloned.1.call-done = f32[256,512]{1,0:T(8,128)} async-done(((f32[2048,512]{1,0:T(8,128)}), f32[256,512]{1,0:T(8,128)}) %reduce-scatter.17.cloned.1.call-update) | async-done | bytes 524304 | tf_op jit(solution)/shard_map/reduce_scatter | solution.py:246
  895.6 193.0 %reduce-scatter.19.cloned.1.call-done = f32[256,1368]{0,1:T(8,128)} async-done(((f32[2048,1368]{0,1:T(8,128)}), f32[256,1368]{0,1:T(8,128)}) %reduce-scatter.19.cloned.1.call-update) | async-done | bytes 1400848 | tf_op jit(solution)/shard_map/reduce_scatter | solution.py:204
  1088.6 192.8 %reduce-scatter.21.cloned.1.call-done = f32[256,1368]{0,1:T(8,128)} async-done(((f32[2048,1368]{0,1:T(8,128)}), f32[256,1368]{0,1:T(8,128)}) %reduce-scatter.21.cloned.1.call-update) | async-done | bytes 1400848 | tf_op jit(solution)/shard_map/reduce_scatter | solution.py:205
  1281.5 193.2 %reduce-scatter.23.cloned.1.call-done = f32[256,1368]{0,1:T(8,128)} async-done(((f32[2048,1368]{0,1:T(8,128)}), f32[256,1368]{0,1:T(8,128)}) %reduce-scatter.23.cloned.1.call-update) | async-done | bytes 1400848 | tf_op jit(solution)/shard_map/reduce_scatter | solution.py:206
  (161 shorter events, 14.7 us)
Async XLA Ops:
  7.2 26.3 %copy-start = (bf16[2048,512]{1,0:T(8,128)(2,1)S(1)}, bf16[2048,512]{1,0:T(8,128)(2,1)}, u32[]{:S(2)}) copy-start(bf16[2048,512]{1,0:T(8,128)(2,1)} %param.23) | copy-start | bytes 6291460
  7.2 115.4 %all-reduce.10.cloned.1.call-start = ((), (), s32[]{:S(2)}) async-start(), calls=%async_computation.8 | async-start | bytes 8388608 | tf_op jit(solution)/shard_map/psum | solution.py:164
  9.2 4.5 copy-start.6
  9.2 4.5 copy-start.20
  29.3 2.0 copy-start.12
  29.3 2.0 copy-start.14
  29.3 2.0 copy-start.27
  30.7 2.0 copy-start.4
  32.7 0.8 copy-start.18
  36.8 192.7 %all-reduce.12.cloned.1.call-start = ((), (), s32[]{:S(2)}) async-start(), calls=%async_computation.9 | async-start | bytes 8388608 | tf_op jit(solution)/shard_map/psum | solution.py:180
  122.6 5.8 slice-start.8
  126.2 2.1 copy-start.2
  126.3 2.5 slice-start.9
  127.0 5.0 slice-start
  128.8 3.2 copy-start.21
  128.8 3.2 slice-start.1
  128.8 9.8 slice-start.4
  132.0 5.5 copy-start.40
  132.0 6.6 slice-start.5
  137.5 1.1 copy-start.36
  143.7 198.3 %all-reduce.14.cloned.1.call-start = ((), (), s32[]{:S(2)}) async-start(), calls=%async_computation.10 | async-start | bytes 8388608 | tf_op jit(solution)/shard_map/psum | solution.py:202
  234.1 1.6 copy-start.11
  234.1 1.6 copy-start.31
  234.7 3.5 copy-start.32
  235.7 5.6 slice-start.6
  238.2 3.1 slice-start.7
  238.2 3.1 copy-start.41
  238.3 3.8 copy-start.42
  238.3 9.3 slice-start.10
  241.4 6.2 copy-start.10
  242.1 5.5 slice-start.11
  247.5 3.7 copy-start.38
  247.5 3.7 copy-start.24
  247.6 3.7 slice-start.2
  247.6 3.7 slice-start.3
  256.3 201.6 %all-reduce.16.cloned.1.call-start = ((), (), s32[]{:S(2)}) async-start(), calls=%async_computation.11 | async-start | bytes 8388608 | tf_op jit(solution)/shard_map/psum | solution.py:239
  342.0 6.3 copy-start.3
  349.5 2.1 copy-start.8
  349.5 3.7 copy-start.5
  349.5 3.8 copy-start.28
  354.3 1.2 copy-start.13
  354.3 1.2 copy-start.15
  356.3 1.9 copy-start.26
  358.2 9.7 copy-start.16
  364.9 3.1 copy-start.9
  364.9 3.5 copy-start.23
  372.0 85.8 %copy-start.33 = (s32[512]{0:T(512)S(1)}, s32[512]{0:T(512)}, u32[]{:S(2)}) copy-start(s32[512]{0:T(512)} %param.16) | copy-start | bytes 6148
  372.0 92.4 %copy-start.7 = (bf16[512,2048]{1,0:T(8,128)(2,1)S(1)}, bf16[512,2048]{1,0:T(8,128)(2,1)}, u32[]{:S(2)}) copy-start(bf16[512,2048]{1,0:T(8,128)(2,1)} %copy-done.6) | copy-start | bytes 6291460
  372.1 171.7 %reduce-scatter.9.cloned.1.call-start = ((), (), s32[]{:S(2)}) async-start(), calls=%async_computation.12 | async-start | bytes 1179648 | tf_op jit(solution)/shard_map/reduce_scatter | solution.py:242
  464.4 154.7 %reduce-scatter.11.cloned.1.call-start = ((), (), s32[]{:S(2)}) async-start(), calls=%async_computation.13 | async-start | bytes 4718592 | tf_op jit(solution)/shard_map/reduce_scatter | solution.py:243
  467.8 243.2 %reduce-scatter.13.cloned.1.call-start = ((), (), s32[]{:S(2)}) async-start(), calls=%async_computation.14 | async-start | bytes 4718592 | tf_op jit(solution)/shard_map/reduce_scatter | solution.py:244
  471.2 1.0 copy-start.17
  471.2 332.4 %reduce-scatter.15.cloned.1.call-start = ((), (), s32[]{:S(2)}) async-start(), calls=%async_computation.15 | async-start | bytes 4718592 | tf_op jit(solution)/shard_map/reduce_scatter | solution.py:245
  475.5 1.0 copy-start.19
  475.5 420.1 %reduce-scatter.17.cloned.1.call-start = ((), (), s32[]{:S(2)}) async-start(), calls=%async_computation.16 | async-start | bytes 4718592 | tf_op jit(solution)/shard_map/reduce_scatter | solution.py:246
  482.2 1.6 copy-start.22
  482.2 2.0 copy-start.39
  482.3 606.4 %reduce-scatter.19.cloned.1.call-start = ((), (), s32[]{:S(2)}) async-start(), calls=%async_computation.17 | async-start | bytes 12607488 | tf_op jit(solution)/shard_map/reduce_scatter | solution.py:204
  490.1 1.4 copy-start.25
  490.1 791.4 %reduce-scatter.21.cloned.1.call-start = ((), (), s32[]{:S(2)}) async-start(), calls=%async_computation.18 | async-start | bytes 12607488 | tf_op jit(solution)/shard_map/reduce_scatter | solution.py:205
  497.2 1.3 copy-start.37
  497.2 977.5 %reduce-scatter.23.cloned.1.call-start = ((), (), s32[]{:S(2)}) async-start(), calls=%async_computation.19 | async-start | bytes 12607488 | tf_op jit(solution)/shard_map/reduce_scatter | solution.py:206
  506.5 968.1 %copy-start.1 = (bf16[2048,512]{1,0:T(8,128)(2,1)S(1)}, bf16[2048,512]{1,0:T(8,128)(2,1)}, u32[]{:S(2)}) copy-start(bf16[2048,512]{1,0:T(8,128)(2,1)} %param.23) | copy-start | bytes 6291460
  506.5 0.8 copy-start.35
  (3 other events, 2.1 us)
Sparse Core Ops, SparseCore 0:
  36.9 85.6 all-reduce.9
  143.8 85.6 all-reduce.11
  256.4 85.6 all-reduce.13
  372.2 85.6 all-reduce.15
  464.6 62.3 reduce-scatter.8
  531.4 87.6 reduce-scatter.10
  623.3 87.6 reduce-scatter.12
  715.7 87.8 reduce-scatter.14
  807.8 87.8 reduce-scatter.16
  900.2 188.3 reduce-scatter.18
  1092.9 188.5 reduce-scatter.20
  1286.1 188.4 reduce-scatter.22
where the time goes:
time: 1490 us; the launch traced here: 1480 us
  waiting for transfers between devices  1270 us (85%)
  matrix products  103 us (7%)
  blocking collectives  32.6 us (2%)
  other arithmetic  32.2 us (2%)
  local copies, waits for them, and re-layouts  25.5 us (2%)
  between operations  17.4 us (1%)
    reduce_scatter x1, waiting for transfers between devices, local(): lax.psum_scatter(grad_w_down, 'dp', scatter_dimension=0, tiled=True)  193 us
    reduce_scatter x1, waiting for transfers between devices, local(): lax.psum_scatter(grad_w_gate, 'dp', scatter_dimension=0, tiled=True)  193 us
    reduce_scatter x1, waiting for transfers between devices, local(): lax.psum_scatter(grad_w_up, 'dp', scatter_dimension=0, tiled=True)  193 us
    reduce_scatter x1, waiting for transfers between devices, local(): lax.psum_scatter(grad_w_value, 'dp', scatter_dimension=0, tiled=True)  92.5 us
    reduce_scatter x1, waiting for transfers between devices, local(): lax.psum_scatter(grad_w_dense, 'dp', scatter_dimension=0, tiled=True)  92.1 us
    reduce_scatter x1, waiting for transfers between devices, local(): lax.psum_scatter(grad_w_key, 'dp', scatter_dimension=0, tiled=True)  91.9 us
    psum x1, waiting for transfers between devices, local(): grad_embedded = deep_alpha * grad_one + lax.psum(input_part, 'mp')  85.7 us
    psum x1, waiting for transfers between devices, local(): grad_hidden = deep_alpha * grad_two + lax.psum(hidden_part, 'mp')  85.7 us
  transfers between devices with their start and end apart: 12, of which 11 were waited for; matrix products, arithmetic and copies ran while one was open for 3% of the time, Pallas kernels for 0%

commit v1 on v0

--- a/solution.py
+++ b/solution.py
@@ -114,6 +114,67 @@
         one_block, (zeros_kv, zeros_kv), (starts, log_total)
     )
     return (grad_queries.reshape(queries.shape), grad_keys, grad_values)
+
+
+def flip_pairs(count, bit):
+    return [(index, index ^ bit) for index in range(count)]
+
+
+def swap(value, axis, count, bit):
+    moved = lax.ppermute(value, axis, flip_pairs(count, bit))
+    return moved
+
+
+def sum_over_groups(part, count):
+    if count != 4:
+        return lax.psum(part, "mp")
+    rows = part.shape[0] // 2
+    core = lax.axis_index("mp") % 2
+    mine = lax.dynamic_slice_in_dim(part, core * rows, rows, 0)
+    other = lax.dynamic_slice_in_dim(part, (1 - core) * rows, rows, 0)
+    half = mine + lax.ppermute(other, "mp", flip_pairs(count, 1))
+    half = half + lax.ppermute(half, "mp", flip_pairs(count, 2))
+    back = lax.ppermute(half, "mp", flip_pairs(count, 1))
+    return jnp.where(
+        core == 0,
+        jnp.concatenate([half, back], axis=0),
+        jnp.concatenate([back, half], axis=0),
+    )
+
+
+def line_scatter(shards, outer):
+    if outer != 4:
+        flat = shards.reshape((-1,) + shards.shape[2:])
+        groups = [[2 * place + parity for place in range(outer)] for parity in range(2)]
+        return lax.psum_scatter(
+            flat, "dp", scatter_dimension=0, tiled=True, axis_index_groups=groups
+        )
+    here = lax.axis_index("dp") // 2
+
+    def shard(place):
+        return lax.dynamic_index_in_dim(shards, jnp.clip(place, 0, outer - 1), 0, keepdims=False)
+
+    from_below = None
+    from_above = None
+    for slot in range(1, outer):
+        up = shard(outer - slot + here)
+        down = shard(slot - outer + here)
+        if from_below is not None:
+            up = up + from_below
+            down = down + from_above
+        up_pairs = [(2 * z + y, 2 * z + 2 + y) for z in range(slot) for y in range(2)]
+        down_pairs = [
+            (2 * (outer - 1 - z) + y, 2 * (outer - 2 - z) + y) for z in range(slot) for y in range(2)
+        ]
+        from_below = lax.ppermute(up, "dp", up_pairs)
+        from_above = lax.ppermute(down, "dp", down_pairs)
+    return shard(here) + from_below + from_above
+
+
+def half_columns(value, parity, outer):
+    rows, width = value.shape
+    parts = value.reshape(rows, outer, 2, width // (2 * outer))
+    return lax.dynamic_index_in_dim(parts, parity, 2, keepdims=False).reshape(rows, width // 2)
 
 
 def local(
@@ -146,10 +207,48 @@
         jnp.bfloat16
     )
     embedded = embedded_low.astype(jnp.float32)
+    their_ids = lax.ppermute(token_ids, "dp", flip_pairs(lax.axis_size("dp"), 1))
+    their_hot = (their_ids[:, None] == jnp.arange(vocab_rows, dtype=jnp.int32)[None, :]).astype(
+        jnp.bfloat16
+    )
+    their_embedded = jnp.dot(their_hot, embedding, preferred_element_type=jnp.float32).astype(
+        jnp.bfloat16
+    )
     cosine, sine = rotary_tables(length, HD)
     prefix = prefix_lengths[0]
+    dp_count = lax.axis_size("dp")
+    mp_count = lax.axis_size("mp")
+    outer = dp_count // 2
+    parity = lax.axis_index("dp") % 2
     own_cluster = cluster_ids[lax.axis_index("dp")]
     seq_weight = 1.0 / jnp.sum((cluster_ids == own_cluster).astype(jnp.float32))
+
+    unit = (prefix_lengths[0] > 0).astype(jnp.float32)
+
+    def exchange(value):
+        return (swap(value.astype(jnp.float32), "dp", dp_count, 1) * unit).astype(jnp.bfloat16)
+
+    def exchange_half(value):
+        theirs = half_columns(value, 1 - parity, outer)
+        if mp_count != 4:
+            return exchange(theirs)
+        rows = length // 2
+        core = lax.axis_index("mp") % 2
+        part = lax.dynamic_slice_in_dim(theirs, core * rows, rows, 0)
+        got = swap(part.astype(jnp.float32), "dp", dp_count, 1) * unit
+        rest = swap(got, "mp", mp_count, 1) * unit
+        got, rest = got.astype(jnp.bfloat16), rest.astype(jnp.bfloat16)
+        return jnp.where(
+            core == 0,
+            jnp.concatenate([got, rest], axis=0),
+            jnp.concatenate([rest, got], axis=0),
+        )
+
+    def pair_product(left, right, left_theirs, right_theirs):
+        both = jnp.einsum(
+            "ld,lf->df", left, right, preferred_element_type=jnp.float32
+        ) + jnp.einsum("ld,lf->df", left_theirs, right_theirs, preferred_element_type=jnp.float32)
+        return line_scatter(both.reshape((outer, -1) + both.shape[1:]), outer)
 
     def project(weight_in):
         return jnp.dot(embedded_low, weight_in, preferred_element_type=jnp.float32).reshape(
@@ -161,8 +260,8 @@
     values_in = project(w_value).astype(jnp.bfloat16)
     attended, log_total = attention_forward(queries, keys_rot, values_in, prefix, row_block)
     attended_low = attended.astype(jnp.bfloat16)
-    branch = lax.psum(
-        jnp.einsum("lh,dh->ld", attended_low, w_dense, preferred_element_type=jnp.float32), "mp"
+    branch = sum_over_groups(
+        jnp.einsum("lh,dh->ld", attended_low, w_dense, preferred_element_type=jnp.float32), mp_count
     )
     residual_one = deep_alpha * embedded + branch
     hidden, norm_one_pull = jax.vjp(layer_norm, residual_one, norm1_gain, norm1_bias)
@@ -177,40 +276,39 @@
 
     activation, gated_pull = jax.vjp(gated_unit, gate_proj, up_proj)
     activation_low = activation.astype(jnp.bfloat16)
-    branch_two = lax.psum(
-        jnp.einsum("lf,df->ld", activation_low, w_down, preferred_element_type=jnp.float32), "mp"
+    branch_two = sum_over_groups(
+        jnp.einsum("lf,df->ld", activation_low, w_down, preferred_element_type=jnp.float32), mp_count
     )
     residual_two = deep_alpha * hidden + branch_two
     final, norm_two_pull = jax.vjp(layer_norm, residual_two, norm2_gain, norm2_bias)
     grad_out = cotangent.astype(jnp.float32) * seq_weight
     grad_two, grad_gain_two, grad_bias_two = norm_two_pull(grad_out)
     grad_branch_two = grad_two.astype(jnp.bfloat16)
-    grad_w_down = jnp.einsum(
-        "ld,lf->df", grad_branch_two, activation_low, preferred_element_type=jnp.float32
-    )
     grad_act = jnp.dot(grad_branch_two, w_down, preferred_element_type=jnp.float32)
     grad_gate, grad_up = gated_pull(grad_act)
     grad_gate_low = grad_gate.astype(jnp.bfloat16)
     grad_up_low = grad_up.astype(jnp.bfloat16)
-    grad_w_gate = jnp.einsum(
-        "ld,lf->df", hidden_low, grad_gate_low, preferred_element_type=jnp.float32
-    )
-    grad_w_up = jnp.einsum("ld,lf->df", hidden_low, grad_up_low, preferred_element_type=jnp.float32)
     hidden_part = jnp.einsum(
         "lf,df->ld", grad_gate_low, w_gate, preferred_element_type=jnp.float32
     ) + jnp.einsum("lf,df->ld", grad_up_low, w_up, preferred_element_type=jnp.float32)
-    grad_hidden = deep_alpha * grad_two + lax.psum(hidden_part, "mp")
-    feed_sums = (
-        lax.psum_scatter(grad_w_gate, "dp", scatter_dimension=0, tiled=True),
-        lax.psum_scatter(grad_w_up, "dp", scatter_dimension=0, tiled=True),
-        lax.psum_scatter(grad_w_down, "dp", scatter_dimension=0, tiled=True),
-        lax.psum_scatter(grad_gain_two, "dp", scatter_dimension=0, tiled=True),
-        lax.psum_scatter(grad_bias_two, "dp", scatter_dimension=0, tiled=True),
-    )
+    grad_hidden = deep_alpha * grad_two + sum_over_groups(hidden_part, mp_count)
+    hidden_half = half_columns(hidden_low, parity, outer)
+    out_w_down = pair_product(
+        half_columns(grad_branch_two, parity, outer),
+        activation_low,
+        exchange_half(grad_branch_two),
+        exchange(activation_low),
+    )
+    hidden_theirs = exchange_half(hidden_low)
+    out_w_gate = pair_product(hidden_half, grad_gate_low, hidden_theirs, exchange(grad_gate_low))
+    out_w_up = pair_product(hidden_half, grad_up_low, hidden_theirs, exchange(grad_up_low))
     grad_one, grad_gain_one, grad_bias_one = norm_one_pull(grad_hidden)
     grad_branch = grad_one.astype(jnp.bfloat16)
-    grad_w_dense = jnp.einsum(
-        "ld,lh->dh", grad_branch, attended_low, preferred_element_type=jnp.float32
+    out_w_dense = pair_product(
+        half_columns(grad_branch, parity, outer),
+        attended_low,
+        exchange_half(grad_branch),
+        exchange(attended_low),
     )
     grad_attended = jnp.dot(grad_branch, w_dense, preferred_element_type=jnp.float32).astype(
         jnp.bfloat16
@@ -222,59 +320,56 @@
     grad_query_lin = rotate(grad_queries, cosine, -sine).astype(jnp.bfloat16).reshape(length, -1)
     grad_key_lin = rotate(grad_keys, cosine, -sine).astype(jnp.bfloat16).reshape(length, -1)
     grad_value_lin = grad_values.astype(jnp.bfloat16).reshape(length, -1)
-    grad_w_query = jnp.einsum(
-        "ld,lh->dh", embedded_low, grad_query_lin, preferred_element_type=jnp.float32
-    )
-    grad_w_key = jnp.einsum(
-        "ld,lh->dh", embedded_low, grad_key_lin, preferred_element_type=jnp.float32
-    )
-    grad_w_value = jnp.einsum(
-        "ld,lh->dh", embedded_low, grad_value_lin, preferred_element_type=jnp.float32
-    )
     input_part = (
         jnp.einsum("lh,dh->ld", grad_query_lin, w_query, preferred_element_type=jnp.float32)
         + jnp.einsum("lh,dh->ld", grad_key_lin, w_key, preferred_element_type=jnp.float32)
         + jnp.einsum("lh,dh->ld", grad_value_lin, w_value, preferred_element_type=jnp.float32)
     )
-    grad_embedded = deep_alpha * grad_one + lax.psum(input_part, "mp")
-    grad_table = 0.1 * jnp.dot(one_hot.astype(jnp.float32).T, grad_embedded, precision=highest)
-    attn_sums = (
-        lax.psum_scatter(grad_table, "dp", scatter_dimension=0, tiled=True),
-        lax.psum_scatter(grad_w_query, "dp", scatter_dimension=0, tiled=True),
-        lax.psum_scatter(grad_w_key, "dp", scatter_dimension=0, tiled=True),
-        lax.psum_scatter(grad_w_value, "dp", scatter_dimension=0, tiled=True),
-        lax.psum_scatter(grad_w_dense, "dp", scatter_dimension=0, tiled=True),
-        lax.psum_scatter(grad_gain_one, "dp", scatter_dimension=0, tiled=True),
-        lax.psum_scatter(grad_bias_one, "dp", scatter_dimension=0, tiled=True),
-    )
-    summed = (
-        attn_sums[0],
-        attn_sums[1],
-        attn_sums[2],
-        attn_sums[3],
-        attn_sums[4],
-        feed_sums[0],
-        feed_sums[1],
-        feed_sums[2],
-        attn_sums[5],
-        attn_sums[6],
-        feed_sums[3],
-        feed_sums[4],
-    )
+    embedded_half = half_columns(embedded_low, parity, outer)
+    embedded_theirs = half_columns(their_embedded, parity, outer)
+    out_w_query = pair_product(
+        embedded_half, grad_query_lin, embedded_theirs, exchange(grad_query_lin)
+    )
+    out_w_key = pair_product(embedded_half, grad_key_lin, embedded_theirs, exchange(grad_key_lin))
+    out_w_value = pair_product(
+        embedded_half, grad_value_lin, embedded_theirs, exchange(grad_value_lin)
+    )
+    own_share = jnp.where(lax.axis_index("mp") == 0, deep_alpha, 0.0)
+    table_part = 0.1 * jnp.dot(
+        one_hot.astype(jnp.float32).T, own_share * grad_one + input_part, precision=highest
+    )
+    table_part = lax.psum_scatter(table_part, "mp", scatter_dimension=1, tiled=True)
+    table_rows = vocab_rows // dp_count
+    width = grad_gain_one.shape[0] // dp_count
+    small = jnp.concatenate(
+        [
+            vector.reshape(dp_count, width)
+            for vector in (grad_gain_one, grad_bias_one, grad_gain_two, grad_bias_two)
+        ]
+        + [table_part.reshape(dp_count, -1)],
+        axis=1,
+    ).reshape(outer, 2, -1)
+    keep = lax.dynamic_index_in_dim(small, parity, 1, keepdims=False)
+    give = lax.dynamic_index_in_dim(small, 1 - parity, 1, keepdims=False)
+    small = keep + lax.ppermute(give, "dp", flip_pairs(dp_count, 1))
+    small = line_scatter(small.reshape(outer, -1, 128), outer).reshape(-1)
+    out_norms = [small[place * width : (place + 1) * width] for place in range(4)]
+    out_table = small[4 * width :].reshape(table_rows, -1)
+    out_table = lax.all_gather(out_table, "mp", axis=1, tiled=True)
     return (
         final.astype(jnp.bfloat16),
-        summed[0],
-        summed[1],
-        summed[2],
-        summed[3],
-        summed[4],
-        summed[5],
-        summed[6],
-        summed[7],
-        summed[8],
-        summed[9],
-        summed[10],
-        summed[11],
+        out_table,
+        out_w_query,
+        out_w_key,
+        out_w_value,
+        out_w_dense,
+        out_w_gate,
+        out_w_up,
+        out_w_down,
+        out_norms[0],
+        out_norms[1],
+        out_norms[2],
+        out_norms[3],
     )
 
 

time: 1490 us -> 1090 us (0.73)
  waiting for transfers between devices: 1270 us -> 365 us
  local copies, waits for them, and re-layouts: 25.5 us -> 245 us
  starting transfers between devices: 0.71 us -> 200 us
  other arithmetic: 32.2 us -> 112 us
  blocking collectives: 32.6 us -> 5.43 us
  matrix products: 103 us -> 127 us
    reduce_scatter x8 -> x1, waiting for transfers between devices: 931 us -> 0.01 us  [local(): lax.psum_scatter(table_part, 'mp', scatter_dimension=1, tiled=True)]
    ppermute x0 -> x72, waiting for transfers between devices: none -> 365 us  [the longest x24 133 us: line_scatter(): from_above = lax.ppermute(down, 'dp', down_pairs)]
    psum x4 -> x0, waiting for transfers between devices: 340 us -> none  [the longest x1 85.7 us: local(): grad_embedded = deep_alpha * grad_one + lax.psum(input_part, 'mp')]
    ppermute x0 -> x72, starting transfers between devices: none -> 200 us  [the longest x24 161 us: line_scatter(): from_above = lax.ppermute(down, 'dp', down_pairs)]
    dynamic_slice x0 -> x10, local copies, waits for them, and re-layouts: none -> 105 us  [the longest x2 68.9 us: shard(): lax.dynamic_index_in_dim(shards, jnp.clip(place, 0, outer - 1), 0, keepdi...]
    unnamed x119 -> x243, local copies, waits for them, and re-layouts: 24.3 us -> 78.5 us
    add x0 -> x41, other arithmetic: none -> 54 us  [the longest x16 17.9 us: line_scatter(): up = up + from_below]
    reshape x0 -> x9, local copies, waits for them, and re-layouts: none -> 47.5 us  [the longest x3 23.8 us: pair_product(): return line_scatter(both.reshape((outer, -1) + both.shape[1:]), outer)]
  transfers between devices with their start and end apart: 12 -> 73, of which waited for: 11 -> 26; matrix products, arithmetic and copies ran while one was open for 3% -> 38% of each run, Pallas kernels for 0% -> 0%
where the time goes in v1:
time: 1090 us; the launch traced here: 1070 us
  waiting for transfers between devices  365 us (33%)
  local copies, waits for them, and re-layouts  245 us (22%)
  starting transfers between devices  200 us (18%)
  matrix products  127 us (12%)
  other arithmetic  112 us (10%)
  between operations  17.7 us (2%)
    ppermute x24, starting transfers between devices, line_scatter(): from_above = lax.ppermute(down, 'dp', down_pairs)  161 us
    ppermute x24, waiting for transfers between devices, line_scatter(): from_above = lax.ppermute(down, 'dp', down_pairs)  133 us
    ppermute x3, waiting for transfers between devices, sum_over_groups(): half = half + lax.ppermute(half, 'mp', flip_pairs(count, 2))  94.3 us
    ppermute x13, waiting for transfers between devices, swap(): moved = lax.ppermute(value, axis, flip_pairs(count, bit))  91.9 us
    unnamed x243, local copies, waits for them, and re-layouts  78.5 us
    dynamic_slice x2, local copies, waits for them, and re-layouts, shard(): lax.dynamic_index_in_dim(shards, jnp.clip(place, 0, outer - 1), 0, keepdi...  68.9 us
    ppermute x24, waiting for transfers between devices, line_scatter(): from_below = lax.ppermute(up, 'dp', up_pairs)  30.4 us
    dynamic_slice x4, local copies, waits for them, and re-layouts, half_columns(): lax.dynamic_index_in_dim(parts, parity, 2, keepdims=False)  30 us
  transfers between devices with their start and end apart: 73, of which 26 were waited for; matrix products, arithmetic and copies ran while one was open for 38% of the time, Pallas kernels for 0%

profile of v1, /device:TPU:30, one launch (start us, length us, event | category | flops | bytes accessed | tf_op | source)
XLA Modules:
  0.0 1071.2 jit_solution(17202128835225868096)
XLA Ops:
  51.7 47.1 %collective-permute-done.1 = f32[256,2048]{1,0:T(8,128)S(1)} collective-permute-done((f32[256,2048]{1,0:T(8,128)S(1)}, f32[256,2048]{1,0:T(8,128)S(1)}, u32[]{:S(2)}, u32[]{:S(2)}) %collective-permute-start.1) | collective-permute-done | bytes 2097184 | tf_op jit(solution)/shard_map/ppermute | solution.py:136
  104.9 5.0 fusion.94
  116.1 6.0 fusion.83
  131.2 47.1 %collective-permute-done.4 = f32[256,2048]{1,0:T(8,128)S(1)} collective-permute-done((f32[256,2048]{1,0:T(8,128)S(1)}, f32[256,2048]{1,0:T(8,128)S(1)}, u32[]{:S(2)}, u32[]{:S(2)}) %collective-permute-start.4) | collective-permute-done | bytes 2097184 | tf_op jit(solution)/shard_map/ppermute | solution.py:136
  180.0 5.0 reshape.364
  185.0 8.6 constant_dynamic-slice_fusion.23
  193.6 5.8 copy.109
  212.3 15.5 %collective-permute-done.47 = f32[256,1024]{0,1:T(8,128)} collective-permute-done((f32[256,1024]{0,1:T(8,128)}, f32[256,1024]{0,1:T(8,128)}, u32[]{:S(2)}, u32[]{:S(2)}) %collective-permute-start.47) | collective-permute-done | bytes 1048608 | tf_op jit(solution)/shard_map/ppermute | solution.py:124
  245.0 4.7 reshape.369
  249.7 12.9 %fusion.84 = (f32[512,1368]{0,1:T(8,128)}, bf16[512,1368]{0,1:T(8,128)(2,1)}, f32[512,1368]{0,1:T(8,128)}, bf16[512,1368]{0,1:T(8,128)(2,1)S(1)}) fusion(f32[512,1368]{0,1:T(8,128)} %copy-done.100, f32[512,1368]{0,1:T(8,128)} %get-tuple-element.168, f32[1368]{0:T(1024)S(1)} %fusion.71, bf16[512,2048]{1,0:T(8,128)(2,1)} %add_convert_fusion.2, ...), kind=kOutput, calls=%fused_computation.278 | convolution fusion | flops 2887815168 | bytes 21714272 | tf_op jit(solution)/shard_map/dot_general | solution.py:287
  263.6 7.8 fusion.104
  271.5 6.3 constant_dynamic-slice_fusion.7
  277.8 5.8 copy.111
  286.3 7.2 convolution_add_fusion.3
  302.8 5.8 copy.108
  311.5 5.7 fusion.112
  324.1 5.8 copy.110
  339.2 6.0 convolution_add_fusion
  345.2 7.8 reshape.372
  353.1 20.8 %collective-permute-done.49 = f32[512,1368]{0,1:T(8,128)} collective-permute-done((f32[512,1368]{0,1:T(8,128)}, f32[512,1368]{0,1:T(8,128)}, u32[]{:S(2)}, u32[]{:S(2)}) %collective-permute-start.49) | collective-permute-done | bytes 2801696 | tf_op jit(solution)/shard_map/ppermute | solution.py:124
  373.9 7.5 convolution_add_fusion.2
  381.4 8.2 reshape.367
  389.7 23.5 %constant_dynamic-slice_fusion.22 = (f32[1,256,1368]{1,0,2:T(1,128)}, f32[1,256,1368]{1,0,2:T(1,128)S(1)}, f32[1,256,1368]{1,0,2:T(1,128)}, f32[1,256,1368]{1,0,...) fusion(f32[4,256,1368]{1,0,2:T(4,128)} %reshape.367, s32[]{:T(128)S(6)} %min.71, ...), kind=kLoop, calls=%fused_computation.227 | loop fusion | bytes 19611676 | tf_op jit(solution)/shard_map/jit(dynamic_index_in_dim)/dynamic_slice | solution.py:155
  421.0 12.5 %collective-permute-done.56 = f32[512,1368]{0,1:T(8,128)} collective-permute-done((f32[512,1368]{0,1:T(8,128)}, f32[512,1368]{0,1:T(8,128)}, u32[]{:S(2)}, u32[]{:S(2)}) %collective-permute-start.56) | collective-permute-done | bytes 2801696 | tf_op jit(solution)/shard_map/ppermute | solution.py:124
  433.5 5.9 convolution_add_fusion.1
  439.4 7.8 reshape.368
  447.1 45.4 %constant_dynamic-slice_fusion.6 = (f32[1,256,1368]{1,0,2:T(1,128)}, f32[1,256,1368]{1,0,2:T(1,128)}, f32[1,256,1368]{1,0,2:T(1,128)}, f32[1,256,1368]{1,0,2:T(1...) fusion(f32[4,256,1368]{1,0,2:T(4,128)} %reshape.372, ...), kind=kLoop, calls=%fused_computation.211 | loop fusion | bytes 39223324 | tf_op jit(solution)/shard_map/jit(dynamic_index_in_dim)/dynamic_slice | solution.py:155
  498.8 6.4 constant_dynamic-slice_fusion.27
  505.2 5.8 copy.104
  511.0 4.6 copy.105
  536.1 22.8 %collective-permute-done.69 = f32[256,1368]{0,1:T(8,128)S(1)} collective-permute-done((f32[256,1368]{0,1:T(8,128)S(1)}, f32[256,1368]{0,1:T(8,128)S(1)}, u32[]{:S(2)}, u32[]{:S(2)}) %collective-permute-start.69) | collective-permute-done | bytes 1400864 | tf_op jit(solution)/shard_map/ppermute | solution.py:170
  564.9 24.0 %collective-permute-done.54 = f32[256,1368]{0,1:T(8,128)S(1)} collective-permute-done((f32[256,1368]{0,1:T(8,128)S(1)}, f32[256,1368]{0,1:T(8,128)S(1)}, u32[]{:S(2)}, u32[]{:S(2)}) %collective-permute-start.54) | collective-permute-done | bytes 1400864 | tf_op jit(solution)/shard_map/ppermute | solution.py:170
  596.7 22.2 %collective-permute-done.61 = f32[256,1368]{0,1:T(8,128)S(1)} collective-permute-done((f32[256,1368]{0,1:T(8,128)S(1)}, f32[256,1368]{0,1:T(8,128)S(1)}, u32[]{:S(2)}, u32[]{:S(2)}) %collective-permute-start.61) | collective-permute-done | bytes 1400864 | tf_op jit(solution)/shard_map/ppermute | solution.py:170
  618.9 5.5 collective-permute-start.55
  628.4 20.6 %collective-permute-done.70 = f32[256,1368]{0,1:T(8,128)S(1)} collective-permute-done((f32[256,1368]{0,1:T(8,128)S(1)}, f32[256,1368]{0,1:T(8,128)S(1)}, u32[]{:S(2)}, u32[]{:S(2)}) %collective-permute-start.70) | collective-permute-done | bytes 1400864 | tf_op jit(solution)/shard_map/ppermute | solution.py:170
  648.9 5.5 collective-permute-start.62
  658.5 6.0 collective-permute-start.71
  681.8 4.9 reshape.360
  689.6 5.3 fusion.107
  701.4 5.1 fusion.105
  714.9 5.7 fusion.21
  720.7 8.7 constant_dynamic-slice_fusion.25
  729.4 5.8 copy.107
  738.5 5.9 copy.106
  764.0 30.3 %collective-permute-done.68 = f32[256,1368]{0,1:T(8,128)S(1)} collective-permute-done((f32[256,1368]{0,1:T(8,128)S(1)}, f32[256,1368]{0,1:T(8,128)S(1)}, u32[]{:S(2)}, u32[]{:S(2)}) %collective-permute-start.68) | collective-permute-done | bytes 1400864 | tf_op jit(solution)/shard_map/ppermute | solution.py:169
  804.3 20.0 %collective-permute-done.24 = f32[512,512]{0,1:T(8,128)S(1)} collective-permute-done((f32[512,512]{0,1:T(8,128)S(1)}, f32[512,512]{0,1:T(8,128)S(1)}, u32[]{:S(2)}, u32[]{:S(2)}) %collective-permute-start.24) | collective-permute-done | bytes 1048608 | tf_op jit(solution)/shard_map/ppermute | solution.py:124
  824.3 16.5 %collective-permute-start.21 = (f32[256,512]{1,0:T(8,128)}, f32[256,512]{1,0:T(8,128)}, u32[]{:S(2)}, u32[]{:S(2)}) collective-permute-start(f32[256,512]{1,0:T(8,128)} %get-tuple-element.140), channel_id=1, source_target_pairs={{24,16},{28,20},{25,17},{29,21},{26,18},{30,22},{27,19},{31,23}} | collective-permute-start | bytes 1572872 | tf_op jit(solution)/shard_map/ppermute | solution.py:170
  849.3 15.6 %collective-permute-done.38 = f32[256,1024]{0,1:T(8,128)S(1)} collective-permute-done((f32[256,1024]{0,1:T(8,128)S(1)}, f32[256,1024]{0,1:T(8,128)S(1)}, u32[]{:S(2)}, u32[]{:S(2)}) %collective-permute-start.38) | collective-permute-done | bytes 1048608 | tf_op jit(solution)/shard_map/ppermute | solution.py:124
  866.5 17.0 %collective-permute-start.28 = (f32[256,512]{1,0:T(8,128)}, f32[256,512]{1,0:T(8,128)}, u32[]{:S(2)}, u32[]{:S(2)}) collective-permute-start(f32[256,512]{1,0:T(8,128)} %get-tuple-element.136), channel_id=1, source_target_pairs={{24,16},{28,20},{25,17},{29,21},{26,18},{30,22},{27,19},{31,23}} | collective-permute-start | bytes 1572872 | tf_op jit(solution)/shard_map/ppermute | solution.py:170
  904.6 13.3 %collective-permute-start.22 = (f32[256,512]{1,0:T(8,128)}, f32[256,512]{1,0:T(8,128)S(1)}, u32[]{:S(2)}, u32[]{:S(2)}) collective-permute-start(f32[256,512]{1,0:T(8,128)} %get-tuple-element.138), channel_id=1, source_target_pairs={{24,16},{28,20},{16,8},{20,12},{25,17},{29,21},{17,9},{21,13},{26,... | collective-permute-start | bytes 1572872 | tf_op jit(solution)/shard_map/ppermute | solution.py:170
  918.0 23.9 %collective-permute-start.13 = (f32[72,128]{1,0:T(8,128)S(1)}, f32[72,128]{1,0:T(8,128)S(1)}, u32[]{:S(2)}, u32[]{:S(2)}) collective-permute-start(f32[72,128]{1,0:T(8,128)S(1)} %get-tuple-element.158), channel_id=1, source_target_pairs={{24,16},{28,20},{25,17},{29,21},{26,18},{30,22},{27,19},{31,23}} | collective-permute-start | bytes 110600 | tf_op jit(solution)/shard_map/ppermute | solution.py:170
  946.1 4.5 collective-permute-start.14
  955.1 4.9 collective-permute-start.15
  962.2 4.7 collective-permute-start.29
  967.0 12.4 %collective-permute-start.44 = (f32[256,512]{1,0:T(8,128)}, f32[256,512]{1,0:T(8,128)}, u32[]{:S(2)}, u32[]{:S(2)}) collective-permute-start(f32[256,512]{1,0:T(8,128)} %get-tuple-element.126), channel_id=1, source_target_pairs={{24,16},{28,20},{25,17},{29,21},{26,18},{30,22},{27,19},{31,23}} | collective-permute-start | bytes 1572872 | tf_op jit(solution)/shard_map/ppermute | solution.py:170
  981.6 5.4 all_gather.3
  990.2 4.7 collective-permute-start.36
  1001.4 5.8 collective-permute-done.36
  1013.1 5.4 collective-permute-done.23
  1024.8 4.8 collective-permute-done.45
  1031.1 5.0 collective-permute-start.46
  1036.1 4.8 collective-permute-done.30
  1041.9 10.3 collective-permute-done.37
  1053.1 9.4 collective-permute-done.46
  (491 shorter events, 322.1 us)
Async XLA Ops:
  7.2 881.1 %reduce-scatter.2.cloned.1.call-start = ((), (), s32[]{:S(2)}) async-start(), calls=%async_computation.1 | async-start | bytes 1310720 | tf_op jit(solution)/shard_map/reduce_scatter | solution.py:341
  51.1 47.7 %collective-permute-start.1 = (f32[256,2048]{1,0:T(8,128)S(1)}, f32[256,2048]{1,0:T(8,128)S(1)}, u32[]{:S(2)}, u32[]{:S(2)}) collective-permute-start(f32[256,2048]{1,0:T(8,128)S(1)} %dynamic-slice_add_fusion.2), channel_id=1, source_target_pairs={{0,2},{1,3},{2,0},{3,1},{4,6},{5,7},{6,4},{7,5},{8,10},{9,11},{10,... | collective-permute-start | bytes 6291464 | tf_op jit(solution)/shard_map/ppermute | solution.py:136
  130.6 47.7 %collective-permute-start.4 = (f32[256,2048]{1,0:T(8,128)S(1)}, f32[256,2048]{1,0:T(8,128)S(1)}, u32[]{:S(2)}, u32[]{:S(2)}) collective-permute-start(f32[256,2048]{1,0:T(8,128)S(1)} %dynamic-slice_add_fusion.1), channel_id=1, source_target_pairs={{0,2},{1,3},{2,0},{3,1},{4,6},{5,7},{6,4},{7,5},{8,10},{9,11},{10,... | collective-permute-start | bytes 6291464 | tf_op jit(solution)/shard_map/ppermute | solution.py:136
  180.0 50.2 %collective-permute-start.5 = (f32[256,2048]{1,0:T(8,128)}, f32[256,2048]{1,0:T(8,128)}, u32[]{:S(2)}, u32[]{:S(2)}) collective-permute-start(f32[256,2048]{1,0:T(8,128)} %add.481), channel_id=1, source_target_pairs={{0,1},{1,0},{2,3},{3,2},{4,5},{5,4},{6,7},{7,6},{8,9},{9,8},{10,11... | collective-permute-start | bytes 6291464 | tf_op jit(solution)/shard_map/ppermute | solution.py:137
  201.5 26.3 %collective-permute-start.47 = (f32[256,1024]{0,1:T(8,128)}, f32[256,1024]{0,1:T(8,128)}, u32[]{:S(2)}, u32[]{:S(2)}) collective-permute-start(f32[256,1024]{0,1:T(8,128)} %dynamic-slice_convert_fusion.1), channel_id=1, source_target_pairs={{0,4},{4,0},{8,12},{12,8},{16,20},{20,16},{24,28},{28,24},{1,5},{5... | collective-permute-start | bytes 3145736 | tf_op jit(solution)/shard_map/ppermute | solution.py:124
  202.0 94.2 %collective-permute-start.16 = (s32[512]{0:T(512)S(1)}, s32[512]{0:T(512)S(1)}, u32[]{:S(2)}, u32[]{:S(2)}) collective-permute-start(s32[512]{0:T(512)S(1)} %copy-done.94), channel_id=1, source_target_pairs={{0,4},{4,0},{8,12},{12,8},{16,20},{20,16},{24,28},{28,24},{1,5},{5... | collective-permute-start | bytes 6152 | tf_op jit(solution)/shard_map/ppermute | solution.py:210
  211.8 127.5 %collective-permute-start.65 = (f32[512,1368]{0,1:T(8,128)}, f32[512,1368]{0,1:T(8,128)}, u32[]{:S(2)}, u32[]{:S(2)}) collective-permute-start(f32[512,1368]{0,1:T(8,128)} %get-tuple-element.72), channel_id=1, source_target_pairs={{0,4},{4,0},{8,12},{12,8},{16,20},{20,16},{24,28},{28,24},{1,5},{5... | collective-permute-start | bytes 8405000 | tf_op jit(solution)/shard_map/ppermute | solution.py:124
  230.1 78.5 %collective-permute-start.48 = (f32[256,1024]{0,1:T(8,128)}, f32[256,1024]{0,1:T(8,128)}, u32[]{:S(2)}, u32[]{:S(2)}) collective-permute-start(f32[256,1024]{0,1:T(8,128)} %get-tuple-element.77), channel_id=1, source_target_pairs={{0,1},{1,0},{2,3},{3,2},{4,5},{5,4},{6,7},{7,6},{8,9},{9,8},{10,11... | collective-permute-start | bytes 3145736 | tf_op jit(solution)/shard_map/ppermute | solution.py:124
  285.8 31.5 %collective-permute-start.63 = (f32[256,1024]{0,1:T(8,128)}, f32[256,1024]{0,1:T(8,128)}, u32[]{:S(2)}, u32[]{:S(2)}) collective-permute-start(f32[256,1024]{0,1:T(8,128)} %dynamic-slice_convert_fusion), channel_id=1, source_target_pairs={{0,4},{4,0},{8,12},{12,8},{16,20},{20,16},{24,28},{28,24},{1,5},{5... | collective-permute-start | bytes 3145736 | tf_op jit(solution)/shard_map/ppermute | solution.py:124
  296.1 37.8 %collective-permute-start.6 = (f32[256,2048]{1,0:T(8,128)}, f32[256,2048]{1,0:T(8,128)}, u32[]{:S(2)}, u32[]{:S(2)}) collective-permute-start(f32[256,2048]{1,0:T(8,128)} %constant_dynamic-slice_fusion.31), channel_id=1, source_target_pairs={{0,1},{1,0},{2,3},{3,2},{4,5},{5,4},{6,7},{7,6},{8,9},{9,8},{10,11... | collective-permute-start | bytes 6291464 | tf_op jit(solution)/shard_map/ppermute | solution.py:135
  310.0 63.9 %collective-permute-start.49 = (f32[512,1368]{0,1:T(8,128)}, f32[512,1368]{0,1:T(8,128)}, u32[]{:S(2)}, u32[]{:S(2)}) collective-permute-start(f32[512,1368]{0,1:T(8,128)} %get-tuple-element.112), channel_id=1, source_target_pairs={{0,4},{4,0},{8,12},{12,8},{16,20},{20,16},{24,28},{28,24},{1,5},{5... | collective-permute-start | bytes 8405000 | tf_op jit(solution)/shard_map/ppermute | solution.py:124
  319.9 18.0 %collective-permute-start.64 = (f32[256,1024]{0,1:T(8,128)}, f32[256,1024]{0,1:T(8,128)}, u32[]{:S(2)}, u32[]{:S(2)}) collective-permute-start(f32[256,1024]{0,1:T(8,128)} %get-tuple-element.71), channel_id=1, source_target_pairs={{0,1},{1,0},{2,3},{3,2},{4,5},{5,4},{6,7},{7,6},{8,9},{9,8},{10,11... | collective-permute-start | bytes 3145736 | tf_op jit(solution)/shard_map/ppermute | solution.py:124
  329.9 103.5 %collective-permute-start.56 = (f32[512,1368]{0,1:T(8,128)}, f32[512,1368]{0,1:T(8,128)}, u32[]{:S(2)}, u32[]{:S(2)}) collective-permute-start(f32[512,1368]{0,1:T(8,128)} %get-tuple-element.74), channel_id=1, source_target_pairs={{0,4},{4,0},{8,12},{12,8},{16,20},{20,16},{24,28},{28,24},{1,5},{5... | collective-permute-start | bytes 8405000 | tf_op jit(solution)/shard_map/ppermute | solution.py:124
  337.4 181.3 %collective-permute-start.7 = (f32[256,2048]{1,0:T(8,128)}, f32[256,2048]{1,0:T(8,128)}, u32[]{:S(2)}, u32[]{:S(2)}) collective-permute-start(f32[256,2048]{1,0:T(8,128)} %dynamic-slice_add_fusion), channel_id=1, source_target_pairs={{0,2},{1,3},{2,0},{3,1},{4,6},{5,7},{6,4},{7,5},{8,10},{9,11},{10,... | collective-permute-start | bytes 6291464 | tf_op jit(solution)/shard_map/ppermute | solution.py:136
  414.4 108.4 %collective-permute-start.53 = (f32[256,1368]{0,1:T(8,128)}, f32[256,1368]{0,1:T(8,128)}, u32[]{:S(2)}, u32[]{:S(2)}) collective-permute-start(f32[256,1368]{0,1:T(8,128)} %bitcast.243), channel_id=1, source_target_pairs={{24,16},{28,20},{25,17},{29,21},{26,18},{30,22},{27,19},{31,23}} | collective-permute-start | bytes 4202504 | tf_op jit(solution)/shard_map/ppermute | solution.py:170
  419.2 106.0 %collective-permute-start.50 = (f32[256,1368]{0,1:T(8,128)}, f32[256,1368]{0,1:T(8,128)}, u32[]{:S(2)}, u32[]{:S(2)}) collective-permute-start(f32[256,1368]{0,1:T(8,128)} %bitcast.244), channel_id=1, source_target_pairs={{0,8},{4,12},{1,9},{5,13},{2,10},{6,14},{3,11},{7,15}} | collective-permute-start | bytes 4202504 | tf_op jit(solution)/shard_map/ppermute | solution.py:169
  495.2 33.8 %collective-permute-start.60 = (f32[256,1368]{0,1:T(8,128)}, f32[256,1368]{0,1:T(8,128)}, u32[]{:S(2)}, u32[]{:S(2)}) collective-permute-start(f32[256,1368]{0,1:T(8,128)} %bitcast.241), channel_id=1, source_target_pairs={{24,16},{28,20},{25,17},{29,21},{26,18},{30,22},{27,19},{31,23}} | collective-permute-start | bytes 4202504 | tf_op jit(solution)/shard_map/ppermute | solution.py:170
  517.2 17.9 %collective-permute-start.57 = (f32[256,1368]{0,1:T(8,128)S(1)}, f32[256,1368]{0,1:T(8,128)S(1)}, u32[]{:S(2)}, u32[]{:S(2)}) collective-permute-start(f32[256,1368]{0,1:T(8,128)S(1)} %bitcast.295), channel_id=1, source_target_pairs={{0,8},{4,12},{1,9},{5,13},{2,10},{6,14},{3,11},{7,15}} | collective-permute-start | bytes 4202504 | tf_op jit(solution)/shard_map/ppermute | solution.py:169
  518.7 40.2 %collective-permute-start.69 = (f32[256,1368]{0,1:T(8,128)S(1)}, f32[256,1368]{0,1:T(8,128)S(1)}, u32[]{:S(2)}, u32[]{:S(2)}) collective-permute-start(f32[256,1368]{0,1:T(8,128)S(1)} %bitcast.294), channel_id=1, source_target_pairs={{24,16},{28,20},{25,17},{29,21},{26,18},{30,22},{27,19},{31,23}} | collective-permute-start | bytes 4202504 | tf_op jit(solution)/shard_map/ppermute | solution.py:170
  522.8 40.8 %collective-permute-start.66 = (f32[256,1368]{0,1:T(8,128)S(1)}, f32[256,1368]{0,1:T(8,128)S(1)}, u32[]{:S(2)}, u32[]{:S(2)}) collective-permute-start(f32[256,1368]{0,1:T(8,128)S(1)} %bitcast.293), channel_id=1, source_target_pairs={{0,8},{4,12},{1,9},{5,13},{2,10},{6,14},{3,11},{7,15}} | collective-permute-start | bytes 4202504 | tf_op jit(solution)/shard_map/ppermute | solution.py:169
  525.2 133.3 %collective-permute-start.8 = (f32[256,2048]{1,0:T(8,128)S(1)}, f32[256,2048]{1,0:T(8,128)S(1)}, u32[]{:S(2)}, u32[]{:S(2)}) collective-permute-start(f32[256,2048]{1,0:T(8,128)S(1)} %add.489), channel_id=1, source_target_pairs={{0,1},{1,0},{2,3},{3,2},{4,5},{5,4},{6,7},{7,6},{8,9},{9,8},{10,11... | collective-permute-start | bytes 6291464 | tf_op jit(solution)/shard_map/ppermute | solution.py:137
  529.0 59.9 %collective-permute-start.54 = (f32[256,1368]{0,1:T(8,128)S(1)}, f32[256,1368]{0,1:T(8,128)S(1)}, u32[]{:S(2)}, u32[]{:S(2)}) collective-permute-start(f32[256,1368]{0,1:T(8,128)S(1)} %bitcast_add_fusion.10), channel_id=1, source_target_pairs={{24,16},{28,20},{16,8},{20,12},{25,17},{29,21},{17,9},{21,13},{26,... | collective-permute-start | bytes 4202504 | tf_op jit(solution)/shard_map/ppermute | solution.py:170
  535.1 59.6 %collective-permute-start.51 = (f32[256,1368]{0,1:T(8,128)S(1)}, f32[256,1368]{0,1:T(8,128)S(1)}, u32[]{:S(2)}, u32[]{:S(2)}) collective-permute-start(f32[256,1368]{0,1:T(8,128)S(1)} %bitcast_add_fusion.12), channel_id=1, source_target_pairs={{0,8},{4,12},{8,16},{12,20},{1,9},{5,13},{9,17},{13,21},{2,10},{6,... | collective-permute-start | bytes 4202504 | tf_op jit(solution)/shard_map/ppermute | solution.py:169
  558.9 60.0 %collective-permute-start.61 = (f32[256,1368]{0,1:T(8,128)S(1)}, f32[256,1368]{0,1:T(8,128)S(1)}, u32[]{:S(2)}, u32[]{:S(2)}) collective-permute-start(f32[256,1368]{0,1:T(8,128)S(1)} %bitcast_add_fusion.5), channel_id=1, source_target_pairs={{24,16},{28,20},{16,8},{20,12},{25,17},{29,21},{17,9},{21,13},{26,... | collective-permute-start | bytes 4202504 | tf_op jit(solution)/shard_map/ppermute | solution.py:170
  563.6 62.2 %collective-permute-start.58 = (f32[256,1368]{0,1:T(8,128)S(1)}, f32[256,1368]{0,1:T(8,128)S(1)}, u32[]{:S(2)}, u32[]{:S(2)}) collective-permute-start(f32[256,1368]{0,1:T(8,128)S(1)} %bitcast_add_fusion.7), channel_id=1, source_target_pairs={{0,8},{4,12},{8,16},{12,20},{1,9},{5,13},{9,17},{13,21},{2,10},{6,... | collective-permute-start | bytes 4202504 | tf_op jit(solution)/shard_map/ppermute | solution.py:169
  588.9 60.0 %collective-permute-start.70 = (f32[256,1368]{0,1:T(8,128)S(1)}, f32[256,1368]{0,1:T(8,128)S(1)}, u32[]{:S(2)}, u32[]{:S(2)}) collective-permute-start(f32[256,1368]{0,1:T(8,128)S(1)} %bitcast_add_fusion), channel_id=1, source_target_pairs={{24,16},{28,20},{16,8},{20,12},{25,17},{29,21},{17,9},{21,13},{26,... | collective-permute-start | bytes 4202504 | tf_op jit(solution)/shard_map/ppermute | solution.py:170
  594.7 61.1 %collective-permute-start.67 = (f32[256,1368]{0,1:T(8,128)S(1)}, f32[256,1368]{0,1:T(8,128)S(1)}, u32[]{:S(2)}, u32[]{:S(2)}) collective-permute-start(f32[256,1368]{0,1:T(8,128)S(1)} %bitcast_add_fusion.2), channel_id=1, source_target_pairs={{0,8},{4,12},{8,16},{12,20},{1,9},{5,13},{9,17},{13,21},{2,10},{6,... | collective-permute-start | bytes 4202504 | tf_op jit(solution)/shard_map/ppermute | solution.py:169
  618.9 132.3 %collective-permute-start.55 = (f32[256,1368]{0,1:T(8,128)}, f32[256,1368]{0,1:T(8,128)}, u32[]{:S(2)}, u32[]{:S(2)}) collective-permute-start(f32[256,1368]{0,1:T(8,128)} %bitcast_add_fusion.11), channel_id=1, source_target_pairs={{24,16},{28,20},{16,8},{20,12},{8,0},{12,4},{25,17},{29,21},{17,9}... | collective-permute-start | bytes 4202504 | tf_op jit(solution)/shard_map/ppermute | solution.py:170
  625.8 127.3 %collective-permute-start.52 = (f32[256,1368]{0,1:T(8,128)}, f32[256,1368]{0,1:T(8,128)}, u32[]{:S(2)}, u32[]{:S(2)}) collective-permute-start(f32[256,1368]{0,1:T(8,128)} %bitcast_add_fusion.13), channel_id=1, source_target_pairs={{0,8},{4,12},{8,16},{12,20},{16,24},{20,28},{1,9},{5,13},{9,17},{1... | collective-permute-start | bytes 4202504 | tf_op jit(solution)/shard_map/ppermute | solution.py:169
  648.9 109.1 %collective-permute-start.62 = (f32[256,1368]{0,1:T(8,128)}, f32[256,1368]{0,1:T(8,128)}, u32[]{:S(2)}, u32[]{:S(2)}) collective-permute-start(f32[256,1368]{0,1:T(8,128)} %bitcast_add_fusion.6), channel_id=1, source_target_pairs={{24,16},{28,20},{16,8},{20,12},{8,0},{12,4},{25,17},{29,21},{17,9}... | collective-permute-start | bytes 4202504 | tf_op jit(solution)/shard_map/ppermute | solution.py:170
  655.8 102.8 %collective-permute-start.59 = (f32[256,1368]{0,1:T(8,128)}, f32[256,1368]{0,1:T(8,128)}, u32[]{:S(2)}, u32[]{:S(2)}) collective-permute-start(f32[256,1368]{0,1:T(8,128)} %bitcast_add_fusion.8), channel_id=1, source_target_pairs={{0,8},{4,12},{8,16},{12,20},{16,24},{20,28},{1,9},{5,13},{9,17},{1... | collective-permute-start | bytes 4202504 | tf_op jit(solution)/shard_map/ppermute | solution.py:169
  658.5 105.0 %collective-permute-start.71 = (f32[256,1368]{0,1:T(8,128)}, f32[256,1368]{0,1:T(8,128)}, u32[]{:S(2)}, u32[]{:S(2)}) collective-permute-start(f32[256,1368]{0,1:T(8,128)} %bitcast_add_fusion.1), channel_id=1, source_target_pairs={{24,16},{28,20},{16,8},{20,12},{8,0},{12,4},{25,17},{29,21},{17,9}... | collective-permute-start | bytes 4202504 | tf_op jit(solution)/shard_map/ppermute | solution.py:170
  751.2 43.1 %collective-permute-start.68 = (f32[256,1368]{0,1:T(8,128)S(1)}, f32[256,1368]{0,1:T(8,128)S(1)}, u32[]{:S(2)}, u32[]{:S(2)}) collective-permute-start(f32[256,1368]{0,1:T(8,128)S(1)} %copy-done.76), channel_id=1, source_target_pairs={{0,8},{4,12},{8,16},{12,20},{16,24},{20,28},{1,9},{5,13},{9,17},{1... | collective-permute-start | bytes 4202504 | tf_op jit(solution)/shard_map/ppermute | solution.py:169
  753.1 140.7 %collective-permute-start.40 = (f32[512,512]{0,1:T(8,128)}, f32[512,512]{0,1:T(8,128)}, u32[]{:S(2)}, u32[]{:S(2)}) collective-permute-start(f32[512,512]{0,1:T(8,128)} %bitcast_convert_fusion), channel_id=1, source_target_pairs={{0,4},{4,0},{8,12},{12,8},{16,20},{20,16},{24,28},{28,24},{1,5},{5... | collective-permute-start | bytes 3145736 | tf_op jit(solution)/shard_map/ppermute | solution.py:124
  758.1 43.8 %collective-permute-start.17 = (f32[512,512]{0,1:T(8,128)S(1)}, f32[512,512]{0,1:T(8,128)S(1)}, u32[]{:S(2)}, u32[]{:S(2)}) collective-permute-start(f32[512,512]{0,1:T(8,128)S(1)} %copy-done.81), channel_id=1, source_target_pairs={{0,4},{4,0},{8,12},{12,8},{16,20},{20,16},{24,28},{28,24},{1,5},{5... | collective-permute-start | bytes 3145736 | tf_op jit(solution)/shard_map/ppermute | solution.py:124
  758.6 65.7 %collective-permute-start.24 = (f32[512,512]{0,1:T(8,128)S(1)}, f32[512,512]{0,1:T(8,128)S(1)}, u32[]{:S(2)}, u32[]{:S(2)}) collective-permute-start(f32[512,512]{0,1:T(8,128)S(1)} %copy-done.80), channel_id=1, source_target_pairs={{0,4},{4,0},{8,12},{12,8},{16,20},{20,16},{24,28},{28,24},{1,5},{5... | collective-permute-start | bytes 3145736 | tf_op jit(solution)/shard_map/ppermute | solution.py:124
  763.5 83.3 %collective-permute-start.31 = (f32[512,512]{0,1:T(8,128)S(1)}, f32[512,512]{0,1:T(8,128)S(1)}, u32[]{:S(2)}, u32[]{:S(2)}) collective-permute-start(f32[512,512]{0,1:T(8,128)S(1)} %copy-done.79), channel_id=1, source_target_pairs={{0,4},{4,0},{8,12},{12,8},{16,20},{20,16},{24,28},{28,24},{1,5},{5... | collective-permute-start | bytes 3145736 | tf_op jit(solution)/shard_map/ppermute | solution.py:124
  794.3 70.6 %collective-permute-start.38 = (f32[256,1024]{0,1:T(8,128)S(1)}, f32[256,1024]{0,1:T(8,128)S(1)}, u32[]{:S(2)}, u32[]{:S(2)}) collective-permute-start(f32[256,1024]{0,1:T(8,128)S(1)} %copy-done.82), channel_id=1, source_target_pairs={{0,4},{4,0},{8,12},{12,8},{16,20},{20,16},{24,28},{28,24},{1,5},{5... | collective-permute-start | bytes 3145736 | tf_op jit(solution)/shard_map/ppermute | solution.py:124
  803.7 62.9 %collective-permute-start.18 = (f32[256,512]{1,0:T(8,128)S(1)}, f32[256,512]{1,0:T(8,128)S(1)}, u32[]{:S(2)}, u32[]{:S(2)}) collective-permute-start(f32[256,512]{1,0:T(8,128)S(1)} %get-tuple-element.139), channel_id=1, source_target_pairs={{0,8},{4,12},{1,9},{5,13},{2,10},{6,14},{3,11},{7,15}} | collective-permute-start | bytes 1572872 | tf_op jit(solution)/shard_map/ppermute | solution.py:169
  824.3 76.6 %collective-permute-start.21 = (f32[256,512]{1,0:T(8,128)}, f32[256,512]{1,0:T(8,128)}, u32[]{:S(2)}, u32[]{:S(2)}) collective-permute-start(f32[256,512]{1,0:T(8,128)} %get-tuple-element.140), channel_id=1, source_target_pairs={{24,16},{28,20},{25,17},{29,21},{26,18},{30,22},{27,19},{31,23}} | collective-permute-start | bytes 1572872 | tf_op jit(solution)/shard_map/ppermute | solution.py:170
  846.8 37.6 %collective-permute-start.25 = (f32[256,512]{1,0:T(8,128)S(1)}, f32[256,512]{1,0:T(8,128)S(1)}, u32[]{:S(2)}, u32[]{:S(2)}) collective-permute-start(f32[256,512]{1,0:T(8,128)S(1)} %get-tuple-element.135), channel_id=1, source_target_pairs={{0,8},{4,12},{1,9},{5,13},{2,10},{6,14},{3,11},{7,15}} | collective-permute-start | bytes 1572872 | tf_op jit(solution)/shard_map/ppermute | solution.py:169
  864.9 22.5 %collective-permute-start.32 = (f32[256,512]{1,0:T(8,128)S(1)}, f32[256,512]{1,0:T(8,128)S(1)}, u32[]{:S(2)}, u32[]{:S(2)}) collective-permute-start(f32[256,512]{1,0:T(8,128)S(1)} %get-tuple-element.131), channel_id=1, source_target_pairs={{0,8},{4,12},{1,9},{5,13},{2,10},{6,14},{3,11},{7,15}} | collective-permute-start | bytes 1572872 | tf_op jit(solution)/shard_map/ppermute | solution.py:169
  866.5 51.4 %collective-permute-start.28 = (f32[256,512]{1,0:T(8,128)}, f32[256,512]{1,0:T(8,128)}, u32[]{:S(2)}, u32[]{:S(2)}) collective-permute-start(f32[256,512]{1,0:T(8,128)} %get-tuple-element.136), channel_id=1, source_target_pairs={{24,16},{28,20},{25,17},{29,21},{26,18},{30,22},{27,19},{31,23}} | collective-permute-start | bytes 1572872 | tf_op jit(solution)/shard_map/ppermute | solution.py:170
  884.4 69.4 %collective-permute-start.35 = (f32[256,512]{1,0:T(8,128)}, f32[256,512]{1,0:T(8,128)}, u32[]{:S(2)}, u32[]{:S(2)}) collective-permute-start(f32[256,512]{1,0:T(8,128)} %get-tuple-element.132), channel_id=1, source_target_pairs={{24,16},{28,20},{25,17},{29,21},{26,18},{30,22},{27,19},{31,23}} | collective-permute-start | bytes 1572872 | tf_op jit(solution)/shard_map/ppermute | solution.py:170
  891.8 9.9 collective-permute-start.19
  900.2 41.7 %collective-permute-start.26 = (f32[256,512]{1,0:T(8,128)S(1)}, f32[256,512]{1,0:T(8,128)S(1)}, u32[]{:S(2)}, u32[]{:S(2)}) collective-permute-start(f32[256,512]{1,0:T(8,128)S(1)} %copy-done.87), channel_id=1, source_target_pairs={{0,8},{4,12},{8,16},{12,20},{1,9},{5,13},{9,17},{13,21},{2,10},{6,... | collective-permute-start | bytes 1572872 | tf_op jit(solution)/shard_map/ppermute | solution.py:169
  901.0 54.1 %collective-permute-start.33 = (f32[256,512]{1,0:T(8,128)S(1)}, f32[256,512]{1,0:T(8,128)S(1)}, u32[]{:S(2)}, u32[]{:S(2)}) collective-permute-start(f32[256,512]{1,0:T(8,128)S(1)} %copy-done.86), channel_id=1, source_target_pairs={{0,8},{4,12},{8,16},{12,20},{1,9},{5,13},{9,17},{13,21},{2,10},{6,... | collective-permute-start | bytes 1572872 | tf_op jit(solution)/shard_map/ppermute | solution.py:169
  904.6 83.1 %collective-permute-start.22 = (f32[256,512]{1,0:T(8,128)}, f32[256,512]{1,0:T(8,128)S(1)}, u32[]{:S(2)}, u32[]{:S(2)}) collective-permute-start(f32[256,512]{1,0:T(8,128)} %get-tuple-element.138), channel_id=1, source_target_pairs={{24,16},{28,20},{16,8},{20,12},{25,17},{29,21},{17,9},{21,13},{26,... | collective-permute-start | bytes 1572872 | tf_op jit(solution)/shard_map/ppermute | solution.py:170
  918.0 26.9 %collective-permute-start.13 = (f32[72,128]{1,0:T(8,128)S(1)}, f32[72,128]{1,0:T(8,128)S(1)}, u32[]{:S(2)}, u32[]{:S(2)}) collective-permute-start(f32[72,128]{1,0:T(8,128)S(1)} %get-tuple-element.158), channel_id=1, source_target_pairs={{24,16},{28,20},{25,17},{29,21},{26,18},{30,22},{27,19},{31,23}} | collective-permute-start | bytes 110600 | tf_op jit(solution)/shard_map/ppermute | solution.py:170
  944.8 66.9 %collective-permute-start.20 = (f32[256,512]{1,0:T(8,128)}, f32[256,512]{1,0:T(8,128)S(1)}, u32[]{:S(2)}, u32[]{:S(2)}) collective-permute-start(f32[256,512]{1,0:T(8,128)} %get-tuple-element.137), channel_id=1, source_target_pairs={{0,8},{4,12},{8,16},{12,20},{16,24},{20,28},{1,9},{5,13},{9,17},{1... | collective-permute-start | bytes 1572872 | tf_op jit(solution)/shard_map/ppermute | solution.py:169
  952.3 27.2 %collective-permute-start.41 = (f32[256,512]{1,0:T(8,128)}, f32[256,512]{1,0:T(8,128)}, u32[]{:S(2)}, u32[]{:S(2)}) collective-permute-start(f32[256,512]{1,0:T(8,128)} %get-tuple-element.125), channel_id=1, source_target_pairs={{0,8},{4,12},{1,9},{5,13},{2,10},{6,14},{3,11},{7,15}} | collective-permute-start | bytes 1572872 | tf_op jit(solution)/shard_map/ppermute | solution.py:169
  955.1 11.9 %collective-permute-start.15 = (f32[72,128]{1,0:T(8,128)S(1)}, f32[72,128]{1,0:T(8,128)S(1)}, u32[]{:S(2)}, u32[]{:S(2)}) collective-permute-start(f32[72,128]{1,0:T(8,128)S(1)} %bitcast_add_fusion.37), channel_id=1, source_target_pairs={{24,16},{28,20},{16,8},{20,12},{8,0},{12,4},{25,17},{29,21},{17,9}... | collective-permute-start | bytes 110600 | tf_op jit(solution)/shard_map/ppermute | solution.py:170
  962.2 35.9 %collective-permute-start.29 = (f32[256,512]{1,0:T(8,128)}, f32[256,512]{1,0:T(8,128)}, u32[]{:S(2)}, u32[]{:S(2)}) collective-permute-start(f32[256,512]{1,0:T(8,128)} %get-tuple-element.134), channel_id=1, source_target_pairs={{24,16},{28,20},{16,8},{20,12},{25,17},{29,21},{17,9},{21,13},{26,... | collective-permute-start | bytes 1572872 | tf_op jit(solution)/shard_map/ppermute | solution.py:170
  967.0 23.3 %collective-permute-start.44 = (f32[256,512]{1,0:T(8,128)}, f32[256,512]{1,0:T(8,128)}, u32[]{:S(2)}, u32[]{:S(2)}) collective-permute-start(f32[256,512]{1,0:T(8,128)} %get-tuple-element.126), channel_id=1, source_target_pairs={{24,16},{28,20},{25,17},{29,21},{26,18},{30,22},{27,19},{31,23}} | collective-permute-start | bytes 1572872 | tf_op jit(solution)/shard_map/ppermute | solution.py:170
  980.9 14.0 %collective-permute-start.42 = (f32[256,512]{1,0:T(8,128)S(1)}, f32[256,512]{1,0:T(8,128)S(1)}, u32[]{:S(2)}, u32[]{:S(2)}) collective-permute-start(f32[256,512]{1,0:T(8,128)S(1)} %bitcast_add_fusion.17), channel_id=1, source_target_pairs={{0,8},{4,12},{8,16},{12,20},{1,9},{5,13},{9,17},{13,21},{2,10},{6,... | collective-permute-start | bytes 1572872 | tf_op jit(solution)/shard_map/ppermute | solution.py:169
  987.7 43.4 %collective-permute-start.27 = (f32[256,512]{1,0:T(8,128)}, f32[256,512]{1,0:T(8,128)S(1)}, u32[]{:S(2)}, u32[]{:S(2)}) collective-permute-start(f32[256,512]{1,0:T(8,128)} %get-tuple-element.133), channel_id=1, source_target_pairs={{0,8},{4,12},{8,16},{12,20},{16,24},{20,28},{1,9},{5,13},{9,17},{1... | collective-permute-start | bytes 1572872 | tf_op jit(solution)/shard_map/ppermute | solution.py:169
  990.2 17.0 %collective-permute-start.36 = (f32[256,512]{1,0:T(8,128)S(1)}, f32[256,512]{1,0:T(8,128)S(1)}, u32[]{:S(2)}, u32[]{:S(2)}) collective-permute-start(f32[256,512]{1,0:T(8,128)S(1)} %copy-done.89), channel_id=1, source_target_pairs={{24,16},{28,20},{16,8},{20,12},{25,17},{29,21},{17,9},{21,13},{26,... | collective-permute-start | bytes 1572872 | tf_op jit(solution)/shard_map/ppermute | solution.py:170
  995.0 23.5 %collective-permute-start.23 = (f32[256,512]{1,0:T(8,128)S(1)}, f32[256,512]{1,0:T(8,128)S(1)}, u32[]{:S(2)}, u32[]{:S(2)}) collective-permute-start(f32[256,512]{1,0:T(8,128)S(1)} %bitcast_add_fusion.31), channel_id=1, source_target_pairs={{24,16},{28,20},{16,8},{20,12},{8,0},{12,4},{25,17},{29,21},{17,9}... | collective-permute-start | bytes 1572872 | tf_op jit(solution)/shard_map/ppermute | solution.py:170
  998.2 31.5 %collective-permute-start.45 = (f32[256,512]{1,0:T(8,128)S(1)}, f32[256,512]{1,0:T(8,128)S(1)}, u32[]{:S(2)}, u32[]{:S(2)}) collective-permute-start(f32[256,512]{1,0:T(8,128)S(1)} %get-tuple-element.124), channel_id=1, source_target_pairs={{24,16},{28,20},{16,8},{20,12},{25,17},{29,21},{17,9},{21,13},{26,... | collective-permute-start | bytes 1572872 | tf_op jit(solution)/shard_map/ppermute | solution.py:170
  1007.2 33.7 %collective-permute-start.30 = (f32[256,512]{1,0:T(8,128)S(1)}, f32[256,512]{1,0:T(8,128)S(1)}, u32[]{:S(2)}, u32[]{:S(2)}) collective-permute-start(f32[256,512]{1,0:T(8,128)S(1)} %bitcast_add_fusion.26), channel_id=1, source_target_pairs={{24,16},{28,20},{16,8},{20,12},{8,0},{12,4},{25,17},{29,21},{17,9}... | collective-permute-start | bytes 1572872 | tf_op jit(solution)/shard_map/ppermute | solution.py:170
  1011.8 30.1 %collective-permute-start.34 = (f32[256,512]{1,0:T(8,128)S(1)}, f32[256,512]{1,0:T(8,128)S(1)}, u32[]{:S(2)}, u32[]{:S(2)}) collective-permute-start(f32[256,512]{1,0:T(8,128)S(1)} %copy-done.88), channel_id=1, source_target_pairs={{0,8},{4,12},{8,16},{12,20},{16,24},{20,28},{1,9},{5,13},{9,17},{1... | collective-permute-start | bytes 1572872 | tf_op jit(solution)/shard_map/ppermute | solution.py:169
  1018.4 33.7 %collective-permute-start.37 = (f32[256,512]{1,0:T(8,128)S(1)}, f32[256,512]{1,0:T(8,128)S(1)}, u32[]{:S(2)}, u32[]{:S(2)}) collective-permute-start(f32[256,512]{1,0:T(8,128)S(1)} %bitcast_add_fusion.21), channel_id=1, source_target_pairs={{24,16},{28,20},{16,8},{20,12},{8,0},{12,4},{25,17},{29,21},{17,9}... | collective-permute-start | bytes 1572872 | tf_op jit(solution)/shard_map/ppermute | solution.py:170
  1029.7 23.4 %collective-permute-start.43 = (f32[256,512]{1,0:T(8,128)S(1)}, f32[256,512]{1,0:T(8,128)S(1)}, u32[]{:S(2)}, u32[]{:S(2)}) collective-permute-start(f32[256,512]{1,0:T(8,128)S(1)} %get-tuple-element.123), channel_id=1, source_target_pairs={{0,8},{4,12},{8,16},{12,20},{16,24},{20,28},{1,9},{5,13},{9,17},{1... | collective-permute-start | bytes 1572872 | tf_op jit(solution)/shard_map/ppermute | solution.py:169
  1031.1 31.4 %collective-permute-start.46 = (f32[256,512]{1,0:T(8,128)S(1)}, f32[256,512]{1,0:T(8,128)S(1)}, u32[]{:S(2)}, u32[]{:S(2)}) collective-permute-start(f32[256,512]{1,0:T(8,128)S(1)} %bitcast_add_fusion.16), channel_id=1, source_target_pairs={{24,16},{28,20},{16,8},{20,12},{8,0},{12,4},{25,17},{29,21},{17,9}... | collective-permute-start | bytes 1572872 | tf_op jit(solution)/shard_map/ppermute | solution.py:170
  (118 other events, 1549.1 us)
Sparse Core Ops, SparseCore 0:
  720.8 38.2 reduce-scatter.1

commit v2 on v0

--- a/solution.py
+++ b/solution.py
@@ -1,8 +1,11 @@
+import functools
 import math
 
 import jax
 import jax.numpy as jnp
 from jax import lax
+from jax.experimental import pallas as pl
+from jax.experimental.pallas import tpu as pltpu
 from jax.sharding import PartitionSpec as P
 
 HD = 128
@@ -116,7 +119,7 @@
     return (grad_queries.reshape(queries.shape), grad_keys, grad_values)
 
 
-def local(
+def local_general(
     token_ids,
     prefix_lengths,
     cluster_ids,
@@ -278,9 +281,822 @@
     )
 
 
+LINE = 4
+MESH = pl.DeviceIdType.MESH
+CHUNKS = 4
+LOW = jnp.bfloat16
+FULL = jnp.float32
+TANH_SCALE = math.sqrt(2.0 / math.pi)
+
+
+def dot(left, right):
+    return jnp.dot(left, right, preferred_element_type=FULL)
+
+
+def dot_nt(left, right):
+    return lax.dot_general(left, right, (((1,), (1,)), ((), ())), preferred_element_type=FULL)
+
+
+def dot_tn(left, right):
+    return lax.dot_general(left, right, (((0,), (0,)), ((), ())), preferred_element_type=FULL)
+
+
+def split_low(value):
+    high = value.astype(LOW)
+    return high, (value - high.astype(FULL)).astype(LOW)
+
+
+def row_mean(value):
+    return jnp.mean(value, axis=-1, keepdims=True)
+
+
+def column_tiles(width, tile=512):
+    return [(start, min(tile, width - start)) for start in range(0, width, tile)]
+
+
+def layer_kernel(
+    length, width, local_hidden,
+    prefix_ref, weight_ref, ids_col, ids_row, emb, tab, cos_ref, sin_ref, norms, w_dense_hbm, w_gate_hbm, w_up_hbm,
+    w_down_hbm, cot_hbm,
+    block_out, out_gate, out_up, out_down, out_dense, out_sums,
+    r_act, r_y, r_cols, r_att, xhat_park, grad_two_park, dnx, r_dny, dnv, r_dnz, r_rs, r_rsd,
+    parts, core_in, x_in, back_in, blocks, xbuf, gbuf, obuf, gate_up, grads_low, act_low, send_a, cols_own, cols_send, att_low,
+    heads, w_dense, one_hot, rstd_one, vectors, sums, sums_y, sums_below, sums_above, sums_other,
+    core_s, core_r, x_s, x_r, back_s, back_r, act_s, act_r, cols_s, cols_r, fwd_s, fwd_r, ys_s, ys_r, gb1_s, gb1_r,
+    att_s, att_r, dny_s, dny_r, dnz_s, dnz_r, rs_s, rs_r, sums_s, sums_r, load_sem, weight_sem,
+):
+    dp, mp = lax.axis_index("dp"), lax.axis_index("mp")
+    z, y = lax.div(dp, 2), lax.rem(dp, 2)
+    x, core = lax.div(mp, 2), lax.rem(mp, 2)
+    half = lax.rem(z, 2)
+    rows = length // CHUNKS
+    heads_here = heads.shape[1]
+    block = width // (2 * LINE)
+    alpha = jnp.float32(deep_alpha)
+
+    def at(z_to=None, y_to=None, x_to=None, core_to=None):
+        z_to = z if z_to is None else z_to
+        y_to = y if y_to is None else y_to
+        x_to = x if x_to is None else x_to
+        core_to = core if core_to is None else core_to
+        return (2 * z_to + y_to, 2 * x_to + core_to)
+
+    core_peer = at(core_to=1 - core)
+    x_peer = at(x_to=1 - x)
+    y_peer = at(y_to=1 - y)
+    z_pair = z + 1 - 2 * half
+    z_peer = at(z_to=z_pair)
+
+    def remote(source, target, send, receive, device):
+        return pltpu.make_async_remote_copy(
+            src_ref=source, dst_ref=target, send_sem=send, recv_sem=receive,
+            device_id=device, device_id_type=MESH,
+        )
+
+    def load_all(pairs):
+        copies = [
+            pltpu.make_async_copy(source, target, load_sem.at[place])
+            for place, (source, target) in enumerate(pairs)
+        ]
+        for copy in copies:
+            copy.start()
+        return copies
+
+    def moved(pairs):
+        for copy in load_all(pairs):
+            copy.wait()
+
+    barrier = pltpu.get_barrier_semaphore()
+    greeted = [core_peer, x_peer, y_peer] + [at(z_to=lax.rem(z + step, LINE)) for step in range(1, LINE)]
+    for device in greeted:
+        pl.semaphore_signal(barrier, inc=1, device_id=device, device_id_type=MESH)
+
+    def chunk_rows(chunk):
+        return pl.ds(pl.multiple_of(chunk * rows, rows), rows)
+
+    def core_copy(turn, chunk):
+        return remote(
+            parts.at[chunk, 1 - core], core_in.at[chunk], core_s.at[turn, chunk], core_r.at[turn, chunk], core_peer
+        )
+
+    def x_copy(turn, chunk):
+        return remote(
+            parts.at[chunk, core], x_in.at[turn % 2, chunk], x_s.at[turn, chunk], x_r.at[turn, chunk], x_peer
+        )
+
+    def back_copy(turn, chunk):
+        return remote(
+            parts.at[chunk, core], back_in.at[chunk], back_s.at[turn, chunk], back_r.at[turn, chunk], core_peer
+        )
+
+    def send_part(turn, chunk):
+        core_copy(turn, chunk).wait()
+        parts[chunk, core] = parts[chunk, core] + core_in[chunk]
+        x_copy(turn, chunk).start()
+
+    def take_part(turn, chunk):
+        x_copy(turn, chunk).wait()
+        parts[chunk, core] = parts[chunk, core] + x_in[turn % 2, chunk]
+        back = back_copy(turn, chunk)
+        back.start()
+        mine = parts[chunk, core]
+        back.wait()
+        other = back_in[chunk]
+        return jnp.concatenate([jnp.where(core == 0, mine, other), jnp.where(core == 0, other, mine)], axis=1)
+
+    def put_blocks(value):
+        for place in range(2 * LINE):
+            blocks[place] = value[:, place * block : (place + 1) * block]
+
+    def own_pair_blocks(place):
+        return 2 * place + y
+
+    def sent_pair_block(place):
+        return 2 * (2 * core + place) + 1 - y
+
+    def own_z_block(place):
+        return 4 * half + place
+
+    def sent_z_block(place):
+        return 4 * (1 - half) + 2 * core + place
+
+    def keep_columns(kind, chunk, own_block, sent_block, target):
+        for place in range(LINE):
+            piece = blocks[own_block(place)].T.astype(LOW)
+            cols_own[min(kind, 1), place, :, chunk_rows(chunk)] = piece
+        for place in range(2):
+            target[place, chunk] = blocks[sent_block(place)]
+
+    def cols_copy(kind, chunk, device):
+        return remote(
+            cols_send.at[min(kind, 1), :, chunk], r_cols.at[kind, pl.ds(2 * core, 2), chunk],
+            cols_s.at[kind, chunk], cols_r.at[kind, chunk], device,
+        )
+
+    def forward_copy(kind):
+        view = r_cols.at[kind, pl.ds(2 * core, 2)]
+        return remote(view, view, fwd_s.at[kind], fwd_r.at[kind], core_peer)
+
+    def act_copy(chunk):
+        source = send_a.at[lax.div(chunk, 2), pl.ds(pl.multiple_of(lax.rem(chunk, 2) * rows, rows), rows)]
+        return remote(source, r_act.at[chunk_rows(chunk)], act_s.at[chunk], act_r.at[chunk], z_peer)
+
+    def pair_copy(which, chunk):
+        return remote(
+            gate_up.at[which, chunk_rows(chunk)], r_y.at[which, chunk_rows(chunk)],
+            ys_s.at[which, chunk], ys_r.at[which, chunk], y_peer,
+        )
+
+    def every_chunk(body):
+        lax.fori_loop(0, CHUNKS, lambda chunk, carried: (body(chunk), carried)[1], 0)
+
+    column = lax.broadcasted_iota(jnp.int32, (length, length), 1)
+    row = lax.broadcasted_iota(jnp.int32, (length, length), 0)
+    score_scale = 1.0 / math.sqrt(HD)
+
+    def probabilities(queries, keys):
+        visible = (column < prefix_ref[0]) | (column <= row)
+        scores = jnp.where(visible, dot_nt(queries, keys) * score_scale, -1e30)
+        weights = jnp.exp(scores - jnp.max(scores, axis=-1, keepdims=True))
+        return weights / jnp.sum(weights, axis=-1, keepdims=True)
+
+    def turn_by(value, sine):
+        return value * cos_ref[...] + pltpu.roll(value, HD // 2, 1) * sine
+
+    def head_lanes(place, offset=0):
+        return pl.ds(pl.multiple_of(offset + place * HD, HD), HD)
+
+    def attend_head(place, carried):
+        hot = one_hot[...]
+        lin = []
+        for kind in range(3):
+            high, rest = split_low(tab[kind * heads_here + place])
+            lin.append(dot(hot, high) + dot(hot, rest))
+        queries = turn_by(lin[0], sin_ref[...]).astype(LOW)
+        keys = turn_by(lin[1], sin_ref[...]).astype(LOW)
+        values = lin[2].astype(LOW)
+        heads[0, place], heads[1, place], heads[2, place] = queries, keys, values
+        probability = probabilities(queries, keys).astype(LOW)
+        att_low[:, head_lanes(place)] = dot(probability, values).astype(LOW)
+        return carried
+
+    def first_scope(w_gate, w_up, w_down, cotbuf):
+        weight_copies = [
+            pltpu.make_async_copy(source, target, weight_sem.at[place])
+            for place, (source, target) in enumerate(
+                ((w_dense_hbm, w_dense), (w_gate_hbm, w_gate), (w_up_hbm, w_up), (w_down_hbm, w_down))
+            )
+        ]
+        for copy in weight_copies:
+            copy.start()
+        vocab = emb.shape[0]
+        lanes = lax.broadcasted_iota(jnp.int32, (length, vocab), 1)
+        one_hot[...] = jnp.where(ids_col[...] == lanes, 1.0, 0.0).astype(LOW)
+        vectors[...] = jnp.zeros_like(vectors)
+        lax.fori_loop(0, heads_here, attend_head, 0)
+        weight_copies[0].wait()
+        pl.semaphore_wait(barrier, len(greeted))
+
+        def project(chunk):
+            mixed = att_low[chunk_rows(chunk), :]
+            for side in range(2):
+                for start, size in column_tiles(width // 2, 256):
+                    weight = w_dense[side * (width // 2) + start : side * (width // 2) + start + size, :]
+                    parts[chunk, side, :, start : start + size] = dot_nt(mixed, weight)
+            core_copy(0, chunk).start()
+
+        every_chunk(project)
+        every_chunk(lambda chunk: send_part(0, chunk))
+        for copy in weight_copies[1:]:
+            copy.wait()
+
+        def feed_forward(chunk):
+            branch = take_part(0, chunk)
+            residual = alpha * dot(one_hot[chunk_rows(chunk), :], emb[...]) + branch
+            centered = residual - row_mean(residual)
+            rstd = lax.rsqrt(row_mean(centered * centered) + norm_eps)
+            xhat = centered * rstd
+            rstd_one[chunk] = rstd
+            xbuf[...] = xhat
+            park = pltpu.make_async_copy(xbuf, xhat_park.at[chunk], load_sem.at[0])
+            park.start()
+            hidden_low = (xhat * norms[0:1, :] + norms[1:2, :]).astype(LOW)
+            put_blocks(hidden_low.astype(FULL))
+            keep_columns(0, chunk, own_pair_blocks, sent_pair_block, cols_send.at[0])
+            cols_copy(0, chunk, y_peer).start()
+            base = lax.rem(chunk, 2) * rows
+            for start, size in column_tiles(local_hidden):
+                cut = slice(start, start + size)
+                gate = dot(hidden_low, w_gate[:, cut])
+                up = dot(hidden_low, w_up[:, cut])
+                units = mp * local_hidden + start + lax.broadcasted_iota(jnp.int32, (rows, size), 1)
+                used = jnp.where(units < FF_USED, 1.0, 0.0)
+                square = gate * gate
+                bend = jnp.tanh(TANH_SCALE * gate * (1.0 + 0.044715 * square))
+                gelu = 0.5 * gate * (1.0 + bend) * used
+                slope = 0.5 * (1.0 + bend) + 0.5 * gate * (1.0 - bend * bend) * (
+                    TANH_SCALE * (1.0 + 3.0 * 0.044715 * square)
+                )
+                gate_up[0, chunk_rows(chunk), cut] = slope * up * used
+                gate_up[1, chunk_rows(chunk), cut] = gelu
+                active = (gelu * up).astype(LOW)
+                act_low[chunk_rows(chunk), cut] = active
+                send_a[lax.div(chunk, 2), pl.ds(pl.multiple_of(base, rows), rows), cut] = active.astype(FULL)
+            act_copy(chunk).start()
+            active = act_low[chunk_rows(chunk), :]
+            for side in range(2):
+                for start, size in column_tiles(width // 2, 256):
+                    weight = w_down[side * (width // 2) + start : side * (width // 2) + start + size, :]
+                    parts[chunk, side, :, start : start + size] = dot_nt(active, weight)
+            core_copy(1, chunk).start()
+            park.wait()
+            send_part(1, chunk)
+
+        every_chunk(feed_forward)
+
+        def feed_backward(chunk):
+            loads = load_all(
+                ((xhat_park.at[chunk], xbuf), (cot_hbm.at[chunk_rows(chunk)], cotbuf))
+            )
+            branch = take_part(1, chunk)
+            for copy in loads:
+                copy.wait()
+            residual = alpha * (xbuf[...] * norms[0:1, :] + norms[1:2, :]) + branch
+            centered = residual - row_mean(residual)
+            rstd = lax.rsqrt(row_mean(centered * centered) + norm_eps)
+            xhat = centered * rstd
+            obuf[...] = (xhat * norms[2:3, :] + norms[3:4, :]).astype(LOW)
+            grad_out = cotbuf[...].astype(FULL) * weight_ref[...]
+            vectors[2:3, :] += jnp.sum(grad_out * xhat, axis=0, keepdims=True)
+            vectors[3:4, :] += jnp.sum(grad_out, axis=0, keepdims=True)
+            grad_x = grad_out * norms[2:3, :]
+            grad_two = (grad_x - row_mean(grad_x) - xhat * row_mean(grad_x * xhat)) * rstd
+            gbuf[...] = grad_two
+            stores = load_all(
+                ((obuf, block_out.at[chunk_rows(chunk)]), (gbuf, grad_two_park.at[chunk]))
+            )
+            grad_low = grad_two.astype(LOW)
+            put_blocks(grad_low.astype(FULL))
+            keep_columns(1, chunk, own_z_block, sent_z_block, cols_send.at[1])
+            cols_copy(1, chunk, z_peer).start()
+            for start, size in column_tiles(local_hidden):
+                cut = slice(start, start + size)
+                grad_act = dot(grad_low, w_down[:, cut])
+                for which in range(2):
+                    low = (grad_act * gate_up[which, chunk_rows(chunk), cut]).astype(LOW)
+                    grads_low[which, chunk_rows(chunk), cut] = low
+                    gate_up[which, chunk_rows(chunk), cut] = low.astype(FULL)
+            pair_copy(0, chunk).start()
+            grad_gate = grads_low[0, chunk_rows(chunk), :]
+            grad_up = grads_low[1, chunk_rows(chunk), :]
+            for side in range(2):
+                for start, size in column_tiles(width // 2, 256):
+                    cut = slice(side * (width // 2) + start, side * (width // 2) + start + size)
+                    parts[chunk, side, :, start : start + size] = dot_nt(grad_gate, w_gate[cut, :]) + dot_nt(
+                        grad_up, w_up[cut, :]
+                    )
+            core_copy(2, chunk).start()
+            for copy in stores:
+                copy.wait()
+            send_part(2, chunk)
+
+        every_chunk(feed_backward)
+
+    pl.run_scoped(
+        first_scope,
+        pltpu.VMEM((width, local_hidden), LOW),
+        pltpu.VMEM((width, local_hidden), LOW),
+        pltpu.VMEM((width, local_hidden), LOW),
+        pltpu.VMEM((rows, width), LOW),
+    )
+
+    def second_scope(theirs, cols_theirs, att_theirs, send_b, stage, att_send, grad_att, grad_one_own, sums_up, sums_down):
+        def norm_backward(chunk):
+            loads = load_all(((xhat_park.at[chunk], xbuf), (grad_two_park.at[chunk], gbuf)))
+            branch = take_part(2, chunk)
+            for copy in loads:
+                copy.wait()
+            grad_hidden = alpha * gbuf[...] + branch
+            xhat = xbuf[...]
+            vectors[0:1, :] += jnp.sum(grad_hidden * xhat, axis=0, keepdims=True)
+            vectors[1:2, :] += jnp.sum(grad_hidden, axis=0, keepdims=True)
+            grad_x = grad_hidden * norms[0:1, :]
+            grad_one = (grad_x - row_mean(grad_x) - xhat * row_mean(grad_x * xhat)) * rstd_one[chunk]
+            put_blocks(grad_one)
+            for place in range(2):
+                grad_one_own[chunk_rows(chunk), place * block : (place + 1) * block] = blocks[2 * mp + place]
+            grad_low = grad_one.astype(LOW)
+            put_blocks(grad_low.astype(FULL))
+            keep_columns(2, chunk, own_pair_blocks, sent_pair_block, cols_send.at[1])
+            grad_mixed = dot(grad_low, w_dense[...]).astype(LOW)
+            for place in range(heads_here):
+                grad_att[place, chunk_rows(chunk), :] = grad_mixed[:, place * HD : (place + 1) * HD]
+
+        def fetch_columns(kind):
+            forward = forward_copy(kind)
+            forward.start()
+            forward.wait()
+            for pair in range(2):
+                moved(
+                    [(r_cols.at[kind, 2 * pair + place], blocks.at[pl.ds(CHUNKS * place, CHUNKS)]) for place in range(2)]
+                )
+                for place in range(2):
+                    for chunk in range(CHUNKS):
+                        cols_theirs[min(kind, 1), 2 * pair + place, :, chunk * rows : (chunk + 1) * rows] = blocks[
+                            CHUNKS * place + chunk
+                        ].T.astype(LOW)
+
+        def fetch_rows(source, target):
+            size = stage.shape[1]
+            moved([(source.at[pl.ds(size * place, size)], stage.at[place]) for place in range(2)])
+            for place in range(2):
+                target[size * place : size * (place + 1), :] = stage[place].astype(LOW)
+
+        def outer_product(target, kind, place, own, other):
+            left, left_theirs = cols_own[min(kind, 1), place], cols_theirs[min(kind, 1), place]
+            for start, size in column_tiles(own.shape[-1]):
+                cut = slice(start, start + size)
+                target[:, cut] = dot(left, own[:, cut]) + dot(left_theirs, other[:, cut])
+
+        def down_products():
+            for chunk in range(CHUNKS):
+                act_copy(chunk).wait()
+                cols_copy(1, chunk, z_peer).wait()
+            fetch_columns(1)
+            fetch_rows(r_act, theirs.at[0])
+            homes = [send_a.at[0], send_a.at[1], send_b.at[0], send_b.at[1]]
+            copies = []
+            for place in range(LINE):
+                outer_product(homes[place], 1, place, act_low, theirs.at[0])
+                copies.append(pltpu.make_async_copy(homes[place], dnx.at[place], load_sem.at[place]))
+                copies[-1].start()
+            for copy in copies:
+                copy.wait()
+            for place in range(2):
+                down_pair_copy(place).start()
+
+        def down_pair_copy(place):
+            return remote(dnx.at[2 * place + 1 - y], r_dny.at[place], dny_s.at[place], dny_r.at[place], y_peer)
+
+        def down_line_copy(place):
+            goal = 2 * half + place
+            slot = jnp.where(((z == 2) & (goal == 1)) | ((z == 3) & (goal == 2)), 1, 0)
+            return goal != z, remote(
+                dnv.at[place], r_dnz.at[slot], dnz_s.at[place], dnz_r.at[slot], at(z_to=goal)
+            )
+
+        def down_sums():
+            for place in range(2):
+                down_pair_copy(place).wait()
+                moved([(dnx.at[2 * place + y], stage.at[0]), (r_dny.at[place], stage.at[1])])
+                stage[0] = stage[0] + stage[1]
+                moved([(stage.at[0], dnv.at[place])])
+                leaves, copy = down_line_copy(place)
+                pl.when(leaves)(copy.start)
+
+        def down_landed(slot):
+            return remote(dnv.at[0], r_dnz.at[slot], dnz_s.at[0], dnz_r.at[slot], core_peer)
+
+        def down_end():
+            @pl.when((z == 0) | (z == LINE - 1))
+            def _():
+                down_landed(0).wait_recv()
+                moved([(dnv.at[half], stage.at[0]), (r_dnz.at[0], stage.at[1])])
+
+            @pl.when((z > 0) & (z < LINE - 1))
+            def _():
+                down_landed(0).wait_recv()
+                down_landed(1).wait_recv()
+                moved([(r_dnz.at[0], stage.at[0]), (r_dnz.at[1], stage.at[1])])
+
+            stage[0] = stage[0] + stage[1]
+            moved([(stage.at[0], out_down)])
+            for place in range(2):
+                leaves, copy = down_line_copy(place)
+                pl.when(leaves)(copy.wait_send)
+
+        sent = {0: [], 1: []}
+
+        def line_terms(kind):
+            if kind < 2:
+                return 0, grads_low.at[kind], theirs.at[1 + kind], out_gate if kind == 0 else out_up, local_hidden
+            return 2, att_low, att_theirs, out_dense, att_low.shape[1]
+
+        def line_land(kind, slot, way):
+            return r_rs.at[kind, slot - 1, way] if kind < 2 else r_rsd.at[slot - 1, way]
+
+        def cut_to(ref, size):
+            return ref if size == ref.shape[-1] else ref.at[:, pl.ds(0, size)]
+
+        def line_copy(kind, slot, way, home):
+            size = line_terms(kind)[4]
+            goal = jnp.clip(z + 1 - 2 * way, 0, LINE - 1)
+            return remote(
+                cut_to(home, size), line_land(kind, slot, way), rs_s.at[kind, slot - 1, way],
+                rs_r.at[kind, slot - 1, way], at(z_to=goal),
+            )
+
+        def line_slot(kind, slot):
+            column_kind, own, other, _, size = line_terms(kind)
+            for way in range(2):
+                home = (send_a, send_b)[way].at[len(sent[way]) % 2]
+                if len(sent[way]) >= 2:
+                    active, copy = sent[way][-2]
+                    pl.when(active)(copy.wait_send)
+                active = z < slot if way == 0 else z > LINE - 1 - slot
+                inner = z > 0 if way == 0 else z < LINE - 1
+                copy = line_copy(kind, slot, way, home)
+                sent[way].append((active, copy))
+
+                @pl.when(active)
+                def _():
+                    place = LINE - slot + z if way == 0 else slot - LINE + z
+                    target = cut_to(home, size)
+                    outer_product(target, column_kind, place, own, other)
+                    if slot > 1:
+
+                        @pl.when(inner)
+                        def _():
+                            line_copy(kind, slot - 1, way, home).wait_recv()
+                            arrived = cut_to(stage.at[way], size)
+                            moved([(line_land(kind, slot - 1, way), arrived)])
+                            target[...] = target[...] + arrived[...]
+
+                    copy.start()
+
+        def line_end(kind):
+            column_kind, own, other, result, size = line_terms(kind)
+            total, arrived = cut_to(stage.at[0], size), cut_to(stage.at[1], size)
+            outer_product(total, column_kind, z, own, other)
+            for way in range(2):
+
+                @pl.when(z > 0 if way == 0 else z < LINE - 1)
+                def _():
+                    line_copy(kind, LINE - 1, way, send_a.at[0]).wait_recv()
+                    moved([(line_land(kind, LINE - 1, way), arrived)])
+                    total[...] = total[...] + arrived[...]
+
+            moved([(total, result)])
+
+        def attention_backward(place, carried):
+            queries, keys, values = heads[0, place], heads[1, place], heads[2, place]
+            grad_mixed = grad_att[place]
+            probability = probabilities(queries, keys)
+            grad_prob = dot_nt(grad_mixed, values)
+            centre = jnp.sum(grad_prob * probability, axis=-1, keepdims=True)
+            grad_scores = (probability * (grad_prob - centre)).astype(LOW)
+            grad_queries = dot(grad_scores, keys) * score_scale
+            grad_keys = dot_tn(grad_scores, queries) * score_scale
+            grad_values = dot_tn(probability.astype(LOW), grad_mixed)
+            vocab = emb.shape[0]
+            named = lax.broadcasted_iota(jnp.int32, (vocab, length), 0) == ids_row[...]
+            hot_t = jnp.where(named, 1.0, 0.0).astype(LOW)
+            inner = heads_here * HD
+            sums[0, 0:vocab, head_lanes(place)] = dot(hot_t, turn_by(grad_queries, -sin_ref[...]).astype(LOW))
+            sums[0, 0:vocab, head_lanes(place, inner)] = dot(hot_t, turn_by(grad_keys, -sin_ref[...]).astype(LOW))
+            sums[1, 0:vocab, head_lanes(place)] = dot(hot_t, grad_values.astype(LOW))
+            return carried
+
+        def small_sums():
+            lax.fori_loop(0, heads_here, attention_backward, 0)
+            vocab = emb.shape[0]
+            named = lax.broadcasted_iota(jnp.int32, (vocab, length), 0) == ids_row[...]
+            hot_t = jnp.where(named, 1.0, 0.0).astype(LOW)
+            high, rest = split_low(grad_one_own[...])
+            sums[1, 0:vocab, heads_here * HD :] = dot(hot_t, high) + dot(hot_t, rest)
+            for side in range(2):
+                sums[side, vocab:, :] = vectors[:, side * (width // 2) : (side + 1) * (width // 2)]
+            sums_pair().start()
+
+        def sums_pair():
+            return remote(sums.at[1 - y], sums_y, sums_s.at[0], sums_r.at[0], y_peer)
+
+        def sums_line(way):
+            source, target = ((sums_up, sums_below), (sums_down, sums_above))[way]
+            goal = jnp.clip(z + 1 - 2 * way, 0, LINE - 1)
+            return remote(source, target, sums_s.at[1 + way], sums_r.at[1 + way], at(z_to=goal))
+
+        def sums_back():
+            return remote(sums.at[y], sums_other, sums_s.at[3], sums_r.at[3], y_peer)
+
+        def sums_first():
+            sums_pair().wait()
+            sums[y] = sums[y] + sums_y[...]
+
+            @pl.when(z == 0)
+            def _():
+                sums_up[...] = sums[y]
+                sums_line(0).start()
+
+            @pl.when(z == LINE - 1)
+            def _():
+                sums_down[...] = sums[y]
+                sums_line(1).start()
+
+        def sums_middle():
+            @pl.when(z > 0)
+            def _():
+                sums_line(0).wait_recv()
+
+            @pl.when((z > 0) & (z < LINE - 1))
+            def _():
+                sums_up[...] = sums[y] + sums_below[...]
+                sums_line(0).start()
+
+            @pl.when(z < LINE - 1)
+            def _():
+                sums_line(1).wait_recv()
+
+            @pl.when((z > 0) & (z < LINE - 1))
+            def _():
+                sums_down[...] = sums[y] + sums_above[...]
+                sums_line(1).start()
+
+            @pl.when(z > 0)
+            def _():
+                sums[y] = sums[y] + sums_below[...]
+
+            @pl.when(z < LINE - 1)
+            def _():
+                sums[y] = sums[y] + sums_above[...]
+
+            sums_back().start()
+
+        def sums_end():
+            sums_back().wait()
+            pl.when(z < LINE - 1)(sums_line(0).wait_send)
+            pl.when(z > 0)(sums_line(1).wait_send)
+            moved([(sums.at[y], out_sums.at[y]), (sums_other, out_sums.at[1 - y])])
+
+        def rows_copy():
+            return remote(att_send, r_att, att_s, att_r, y_peer)
+
+        down_products()
+        norm_backward(0)
+        norm_backward(1)
+        for chunk in range(CHUNKS):
+            cols_copy(0, chunk, y_peer).wait()
+        fetch_columns(0)
+        for chunk in range(CHUNKS):
+            pair_copy(0, chunk).wait()
+        fetch_rows(r_y.at[0], theirs.at[1])
+        line_slot(0, 1)
+        for chunk in range(CHUNKS):
+            pair_copy(1, chunk).start()
+        norm_backward(2)
+        norm_backward(3)
+        for chunk in range(CHUNKS):
+            cols_copy(2, chunk, y_peer).start()
+        att_send[...] = att_low[...].astype(FULL)
+        rows_copy().start()
+        line_slot(0, 2)
+        small_sums()
+        line_slot(0, 3)
+        sums_first()
+        for chunk in range(CHUNKS):
+            pair_copy(1, chunk).wait()
+        fetch_rows(r_y.at[1], theirs.at[2])
+        line_slot(1, 1)
+        sums_middle()
+        line_end(0)
+        line_slot(1, 2)
+        down_sums()
+        line_slot(1, 3)
+        for chunk in range(CHUNKS):
+            cols_copy(2, chunk, y_peer).wait()
+        fetch_columns(2)
+        rows_copy().wait()
+        moved([(r_att, att_send)])
+        att_theirs[...] = att_send[...].astype(LOW)
+        line_slot(2, 1)
+        line_slot(2, 2)
+        line_end(1)
+        line_slot(2, 3)
+        sums_end()
+        down_end()
+        line_end(2)
+        for way in range(2):
+            for active, copy in sent[way][-2:]:
+                pl.when(active)(copy.wait_send)
+
+    shard = width // (2 * LINE)
+    pl.run_scoped(
+        second_scope,
+        pltpu.VMEM((3, length, local_hidden), LOW),
+        pltpu.VMEM((2, LINE, block, length), LOW),
+        pltpu.VMEM(att_low.shape, LOW),
+        pltpu.VMEM((2, shard, local_hidden), FULL),
+        pltpu.VMEM((2, shard, local_hidden), FULL),
+        pltpu.VMEM(att_low.shape, FULL),
+        pltpu.VMEM((heads_here, length, HD), LOW),
+        pltpu.VMEM((length, 2 * block), FULL),
+        pltpu.VMEM(sums_y.shape, FULL),
+        pltpu.VMEM(sums_y.shape, FULL),
+    )
+
+
+def local_fast(
+    token_ids,
+    prefix_lengths,
+    cluster_ids,
+    embedding,
+    w_query,
+    w_key,
+    w_value,
+    w_dense,
+    w_gate,
+    w_up,
+    w_down,
+    norm1_gain,
+    norm1_bias,
+    norm2_gain,
+    norm2_bias,
+    cotangent,
+):
+    length = token_ids.shape[0]
+    vocab, width = embedding.shape
+    inner = w_query.shape[1]
+    heads_here = inner // HD
+    local_hidden = w_gate.shape[1]
+    rows = length // CHUNKS
+    block = width // (2 * LINE)
+    dp, mp = lax.axis_index("dp"), lax.axis_index("mp")
+    own_cluster = cluster_ids[dp]
+    seq_weight = 1.0 / jnp.sum((cluster_ids == own_cluster).astype(FULL))
+    tables = [
+        dot(embedding, weight).reshape(vocab, heads_here, HD).transpose(1, 0, 2)
+        for weight in (w_query, w_key, w_value)
+    ]
+    cosine, sine = rotary_tables(length, HD)
+    cosine = jnp.concatenate([cosine, cosine], axis=1)
+    sine = jnp.concatenate([-sine, sine], axis=1)
+    norms = jnp.stack([norm1_gain, norm1_bias, norm2_gain, norm2_bias])
+
+    hbm = pl.BlockSpec(memory_space=pl.ANY)
+    vmem = pl.BlockSpec(memory_space=pltpu.VMEM)
+    sums_rows = vocab + 8
+    shapes = [
+        ((length, width), LOW),
+        ((block, local_hidden), FULL),
+        ((block, local_hidden), FULL),
+        ((block, local_hidden), FULL),
+        ((block, inner), FULL),
+        ((2, sums_rows, width // 2), FULL),
+        ((length, local_hidden), FULL),
+        ((2, length, local_hidden), FULL),
+        ((3, LINE, CHUNKS, rows, block), FULL),
+        ((length, inner), FULL),
+        ((CHUNKS, rows, width), FULL),
+        ((CHUNKS, rows, width), FULL),
+        ((LINE, block, local_hidden), FULL),
+        ((2, block, local_hidden), FULL),
+        ((2, block, local_hidden), FULL),
+        ((2, block, local_hidden), FULL),
+        ((2, LINE - 1, 2, block, local_hidden), FULL),
+        ((LINE - 1, 2, block, inner), FULL),
+    ]
+    scratch = [
+        ((CHUNKS, 2, rows, width // 2), FULL),
+        ((CHUNKS, rows, width // 2), FULL),
+        ((2, CHUNKS, rows, width // 2), FULL),
+        ((CHUNKS, rows, width // 2), FULL),
+        ((2 * LINE, rows, block), FULL),
+        ((rows, width), FULL),
+        ((rows, width), FULL),
+        ((rows, width), LOW),
+        ((2, length, local_hidden), FULL),
+        ((2, length, local_hidden), LOW),
+        ((length, local_hidden), LOW),
+        ((2, block, local_hidden), FULL),
+        ((2, LINE, block, length), LOW),
+        ((2, 2, CHUNKS, rows, block), FULL),
+        ((length, inner), LOW),
+        ((3, heads_here, length, HD), LOW),
+        ((width, inner), LOW),
+        ((length, vocab), LOW),
+        ((CHUNKS, rows, 1), FULL),
+        ((8, width), FULL),
+        ((2, sums_rows, width // 2), FULL),
+        ((sums_rows, width // 2), FULL),
+        ((sums_rows, width // 2), FULL),
+        ((sums_rows, width // 2), FULL),
+        ((sums_rows, width // 2), FULL),
+    ]
+    dma = pltpu.SemaphoreType.DMA
+    semaphores = [
+        (3, CHUNKS), (3, CHUNKS), (3, CHUNKS), (3, CHUNKS), (3, CHUNKS), (3, CHUNKS), (CHUNKS,), (CHUNKS,),
+        (3, CHUNKS), (3, CHUNKS), (3,), (3,), (2, CHUNKS), (2, CHUNKS), (1,), (1,),
+        None, None, (2,), (2,), (2,), (2,), (3, LINE - 1, 2), (3, LINE - 1, 2), (4,), (4,), (4,), (4,),
+    ]
+    results = pl.pallas_call(
+        functools.partial(layer_kernel, length, width, local_hidden),
+        out_shape=[jax.ShapeDtypeStruct(shape, dtype) for shape, dtype in shapes],
+        in_specs=[pl.BlockSpec(memory_space=pltpu.SMEM)] + [vmem] * 8 + [hbm] * 5,
+        out_specs=[hbm] * len(shapes),
+        scratch_shapes=[pltpu.VMEM(shape, dtype) for shape, dtype in scratch]
+        + [dma if shape is None else dma(shape) for shape in semaphores],
+        compiler_params=pltpu.CompilerParams(
+            collective_id=0, has_side_effects=True, vmem_limit_bytes=62 * 2**20
+        ),
+    )(
+        prefix_lengths,
+        seq_weight.reshape(1, 1),
+        token_ids.reshape(length, 1),
+        token_ids.reshape(1, length),
+        embedding,
+        jnp.concatenate(tables, axis=0),
+        cosine,
+        sine,
+        norms,
+        w_dense,
+        w_gate,
+        w_up,
+        w_down,
+        cotangent,
+    )
+    block_out, out_gate, out_up, out_down, out_dense, sums = results[:6]
+    sums = jnp.concatenate([sums[0], sums[1]], axis=1)
+    own_columns = lax.dynamic_slice_in_dim(embedding, dp * block, block, 1).astype(FULL)
+    by_token = [sums[:vocab, kind * inner : (kind + 1) * inner] for kind in range(3)]
+    out_lin = [
+        lax.dot_general(
+            own_columns, part, (((0,), (0,)), ((), ())), precision=highest, preferred_element_type=FULL
+        )
+        for part in by_token
+    ]
+    table_rows = vocab // (2 * LINE)
+    mine = lax.dynamic_slice_in_dim(sums, dp * table_rows, table_rows, 0)
+    high = lax.reduce_precision(mine, 8, 7)
+    pieces = jnp.concatenate([high, mine - high], axis=0).astype(LOW)
+    table = sum(
+        dot_nt(pieces[:, kind * inner : (kind + 1) * inner], weight)
+        for kind, weight in enumerate((w_query, w_key, w_value))
+    )
+    table = table[:table_rows] + table[table_rows:]
+    quarter = lax.dynamic_slice_in_dim(table, mp * inner, inner, 1) + deep_alpha * mine[:, 3 * inner :]
+    table = lax.psum(lax.dynamic_update_slice_in_dim(table, quarter, mp * inner, 1), "mp")
+    norm_rows = lax.dynamic_slice_in_dim(sums[vocab : vocab + 4], dp * block, block, 1)
+    return (
+        block_out,
+        0.1 * table,
+        out_lin[0],
+        out_lin[1],
+        out_lin[2],
+        out_dense,
+        out_gate,
+        out_up,
+        out_down,
+        norm_rows[0],
+        norm_rows[1],
+        norm_rows[2],
+        norm_rows[3],
+    )
+
+
 def solution(mesh):
+    fast = mesh.shape["dp"] == 2 * LINE and mesh.shape["mp"] == 4
     return jax.shard_map(
-        local,
+        local_fast if fast else local_general,
         mesh=mesh,
         in_specs=(
             P("dp"),

time: 1490 us -> 627 us (0.42)
  waiting for transfers between devices: 1270 us -> 21.7 us
  Pallas kernels: 0 us -> 512 us
  matrix products: 103 us -> 14.9 us
  blocking collectives: 32.6 us -> 0 us
  other arithmetic: 32.2 us -> 8 us
  local copies, waits for them, and re-layouts: 25.5 us -> 42.4 us
    reduce_scatter x8 -> x0, waiting for transfers between devices: 931 us -> none  [the longest x1 193 us: local(): lax.psum_scatter(grad_w_down, 'dp', scatter_dimension=0, tiled=True)]
    pallas_call x0 -> x1, Pallas kernels: none -> 512 us  [local_fast(): pl.pallas_call(functools.partial(layer_kernel, length, width, local_hidde...]
    psum x4 -> x1, waiting for transfers between devices: 340 us -> 21.7 us  [local_fast(): lax.psum(lax.dynamic_update_slice_in_dim(table, quarter, mp * inner, 1),...]
    dot_general x29 -> x9, matrix products: 103 us -> 14.9 us  [the longest x3 6.49 us: dot(): return jnp.dot(left, right, preferred_element_type=FULL)]
    unnamed x1 -> x0, blocking collectives: 32.6 us -> none
    reduce_sum x10 -> x1, other arithmetic: 24.1 us -> 1.9 us  [local_fast(): seq_weight = 1.0 / jnp.sum((cluster_ids == own_cluster).astype(FULL))]
    unnamed x119 -> x48, local copies, waits for them, and re-layouts: 24.3 us -> 33.4 us
  transfers between devices with their start and end apart: 12 -> 1, of which waited for: 11 -> 1; matrix products, arithmetic and copies ran while one was open for 3% -> 2% of each run, Pallas kernels for 0% -> 0%
where the time goes in v2:
time: 627 us; the launch traced here: 615 us
  Pallas kernels  512 us (82%)
  local copies, waits for them, and re-layouts  42.4 us (7%)
  waiting for transfers between devices  21.7 us (3%)
  between operations  16 us (3%)
  matrix products  14.9 us (2%)
  other arithmetic  8 us (1%)
    pallas_call x1, Pallas kernels, local_fast(): pl.pallas_call(functools.partial(layer_kernel, length, width, local_hidde...  512 us
    unnamed x48, local copies, waits for them, and re-layouts  33.4 us
    psum x1, waiting for transfers between devices, local_fast(): lax.psum(lax.dynamic_update_slice_in_dim(table, quarter, mp * inner, 1),...  21.7 us
  transfers between devices with their start and end apart: 1, of which 1 were waited for; matrix products, arithmetic and copies ran while one was open for 2% of the time, Pallas kernels for 0%

profile of v2, /device:TPU:30, one launch (start us, length us, event | category | flops | bytes accessed | tf_op | source)
XLA Modules:
  0.0 615.2 jit_solution(10822596896856265198)
XLA Ops:
  7.2 0.0 all-reduce.2.cloned.1.call-start
  7.2 1.2 dynamic_slice.15
  8.5 1.9 fusion.28
  10.4 1.0 fusion.10
  11.4 8.3 %copy.42.w_gate_hbm = bf16[2048,1368]{1,0:T(8,128)(2,1)} copy(bf16[2048,1368]{0,1:T(8,128)(2,1)} %param.24) | data formatting | bytes 11206656 | tf_op args[8]
  19.7 8.2 %copy.43.w_up_hbm = bf16[2048,1368]{1,0:T(8,128)(2,1)} copy(bf16[2048,1368]{0,1:T(8,128)(2,1)} %param.25) | data formatting | bytes 11206656 | tf_op args[9]
  27.9 0.0 copy-start
  27.9 0.0 copy-start.1
  27.9 8.4 %copy.44.w_down_hbm = bf16[2048,1368]{1,0:T(8,128)(2,1)} copy(bf16[2048,1368]{0,1:T(8,128)(2,1)} %param.26) | data formatting | bytes 11206656 | tf_op args[10]
  36.3 0.0 copy-done
  36.3 0.0 copy-done.1
  36.3 1.6 fusion.34
  38.0 0.0 copy-start.4
  38.0 1.9 copy.36
  39.9 3.2 fusion.35
  43.1 1.8 copy.38
  44.9 0.0 copy-done.4
  44.9 1.6 fusion.36
  46.6 0.0 copy-start.18
  46.6 0.0 copy-start.19
  46.6 1.1 copy.40
  47.7 0.0 copy-done.15
  47.7 0.9 copy.41.ids_col
  49.9 1.0 pad_maximum_fusion.1
  50.9 0.0 copy-done.10
  50.9 0.0 copy-done.11
  50.9 0.9 pad_maximum_fusion.tab
  51.9 0.0 copy-done.16
  51.9 0.0 copy-done.17
  51.9 0.0 copy-done.18
  51.9 0.0 copy-done.19
  51.9 0.7 pad_maximum_fusion.5.norms
  52.5 512.1 %shard_map.255 = (bf16[512,2048]{1,0:T(8,128)(2,1)}, f32[256,1368]{1,0:T(8,128)}, f32[256,1368]{1,0:T(8,128)}, f32[256,1368]{1,0:T(8,128)}, f32[256,512]{1,0:T(8...) custom-call(s32[1]{0:T(128)S(6)} %copy.55.prefix_ref, ...), custom_call_target="tpu_custom_call" | custom-call | tf_op jit(solution)/shard_map/pallas_call | solution.py:1031
  564.7 0.0 copy-start.2
  564.7 1.4 slice_bitcast_fusion.1
  566.2 0.0 copy-start.3
  566.2 0.0 copy-start.12
  566.2 0.6 copy-done.12
  566.9 0.0 copy-done.2
  566.9 0.7 fusion.20
  567.6 0.3 copy-done.3
  567.9 0.7 convolution_add_fusion.1
  568.6 0.0 copy-done.5
  568.6 0.7 convolution_add_fusion
  569.4 0.0 copy-start.9
  569.4 0.9 fusion.15
  570.3 0.7 copy-done.13
  570.9 0.0 all-reduce.2.cloned.1.call-update
  571.0 2.1 fusion.2
  573.0 2.0 fusion.4
  575.1 2.2 fusion
  577.2 0.6 fusion.33
  577.8 0.0 copy-done.9
  577.8 1.5 copy.45
  579.3 0.0 copy-done.8
  579.3 1.5 copy.46
  580.9 0.0 copy-done.7
  580.9 1.5 copy.47
  582.4 21.7 %all-reduce.2.cloned.1.call-done = f32[16,2048]{1,0:T(8,128)} async-done(((f32[16,2048]{1,0:T(8,128)}), f32[16,2048]{1,0:T(8,128)}) %all-reduce.2.cloned.1.call-update) | async-done | bytes 131088 | tf_op jit(solution)/shard_map/psum | solution.py:1077
  604.1 1.6 broadcast_multiply_fusion
  605.7 0.0 copy-done.6
  605.7 1.3 copy.56
  607.0 0.1 copy-done.14
  607.1 0.8 copy.57
  (16 shorter events, 0.1 us)
Async XLA Ops:
  7.2 596.9 %all-reduce.2.cloned.1.call-start = ((), (), s32[]{:S(2)}) async-start(), calls=%async_computation | async-start | bytes 262144 | tf_op jit(solution)/shard_map/psum | solution.py:1077
  27.9 8.4 %copy-start = (bf16[128,2048]{1,0:T(8,128)(2,1)S(1)}, bf16[128,2048]{1,0:T(8,128)(2,1)}, u32[]{:S(2)}) copy-start(bf16[128,2048]{1,0:T(8,128)(2,1)} %emb.1) | copy-start | bytes 1572868
  27.9 8.4 %copy-start.1 = (bf16[2048,512]{1,0:T(8,128)(2,1)S(1)}, bf16[2048,512]{1,0:T(8,128)(2,1)}, u32[]{:S(2)}) copy-start(bf16[2048,512]{1,0:T(8,128)(2,1)} %param.20) | copy-start | bytes 6291460
  38.0 7.0 %copy-start.4 = (bf16[2048,512]{1,0:T(8,128)(2,1)S(1)}, bf16[2048,512]{1,0:T(8,128)(2,1)}, u32[]{:S(2)}) copy-start(bf16[2048,512]{1,0:T(8,128)(2,1)} %param.22) | copy-start | bytes 6291460
  43.1 4.6 copy-start.15
  46.6 4.4 copy-start.10
  46.6 4.4 copy-start.11
  46.6 5.3 copy-start.16
  46.6 5.3 copy-start.17
  46.6 5.3 copy-start.18
  46.6 5.3 copy-start.19
  564.7 2.2 copy-start.2
  566.2 1.8 copy-start.3
  566.2 0.7 copy-start.12
  566.9 1.8 copy-start.5
  569.4 8.5 %copy-start.9 = (f32[256,1368]{1,0:T(8,128)S(1)}, f32[256,1368]{1,0:T(8,128)}, u32[]{:S(2)}) copy-start(f32[256,1368]{1,0:T(8,128)} %get-tuple-element.44) | copy-start | bytes 4202500
  570.3 0.7 copy-start.13
  575.1 4.3 copy-start.8
  579.3 1.5 copy-start.7
  580.9 24.8 %copy-start.6 = (bf16[512,2048]{1,0:T(8,128)(2,1)S(1)}, bf16[512,2048]{1,0:T(8,128)(2,1)}, u32[]{:S(2)}) copy-start(bf16[512,2048]{1,0:T(8,128)(2,1)} %get-tuple-element.77) | copy-start | bytes 6291460
  605.7 1.4 copy-start.14
Sparse Core Ops, SparseCore 0:
  571.1 32.9 all-reduce.1
